TPU v7x, 32 devices: a whole 2x2x4 slice. The times are simulated.
32 devices in a mesh: groups: 2 (over x), req: 8 (over z, y), tp: 2 (over core).
Axes of the slice: x: 2, y: 2, z: 4, core: 2. Of those that a mesh axis runs over, the one named last changes fastest.
Arguments:
- ssm_state: float32 [128, 16, 16384], P(('groups', 'req'), None, 'tp'), parts along dimension 0, may hold values from -6 to 6
- conv_state: float32 [128, 3, 16384], P(('groups', 'req'), None, 'tp'), parts along dimension 0, may hold values from -6 to 6
- token_input: bfloat16 [128, 2, 16384], P('groups', None, ('tp', 'req')), parts along dimension 0, may hold values from -6 to 6
- gate_input: bfloat16 [128, 2, 16384], P('groups', None, ('tp', 'req')), parts along dimension 0, may hold values from -6 to 6
- conv_weight: float32 [4, 16384], P(None, 'tp'), may hold values from -3 to 3
- conv_bias: float32 [16384], P('tp'), may hold values from -3 to 3
- proj_weight: bfloat16 [16384, 544], P(('tp', 'req')), may hold values from -0.046875 to 0.046875
- dt_weight: bfloat16 [512, 16384], P(None, ('tp', 'req')), may hold values from -0.25 to 0.25
- dt_bias: float32 [16384], P('tp'), may hold values from -3 to 0.5
- decay_log: float32 [16, 16384], P(None, 'tp'), may hold values from 0 to 2.7
- skip_gain: float32 [16384], P('tp'), may hold values from 0.5 to 1.5
- queries: bfloat16 [128, 2, 8192], P(('groups', 'req'), None, 'tp'), parts along dimension 0, may hold values from -6 to 6
- kv_pages: bfloat16 [2, 2048, 16, 1024], P(None, ('groups', 'req'), None, 'tp'), parts along dimension 1, may hold values from -6 to 6
- new_kv: bfloat16 [128, 2, 2, 1024], P(('groups', 'req'), None, None, 'tp'), parts along dimension 0, may hold values from -6 to 6
- page_table: int32 [16, 128], P(('groups', 'req')), parts along dimension 0, may hold values from 0 to 127, each once within a row
- context_len: int32 [128], P(('groups', 'req')), parts along dimension 0, may hold values from 1 to 256
- decode_row: int32 [128], P('groups'), parts along dimension 0, may hold values from 0 to 63, each once
Outputs:
- mamba_out: bfloat16 [128, 2, 16384], P('groups', None, ('tp', 'req')), parts along dimension 0
- attention_out: bfloat16 [128, 2, 8192], P('groups', None, ('tp', 'req')), parts along dimension 0
There are 2 independent parts, one for each index of `groups`. A program takes and returns all parts, laid end to end along the dimension named above; an argument that names none is the same for every part. Nothing has to cross between parts.
Inputs may be any that keep to these rules, and one draw needn't show every extreme that they name: `page_table`: row d lists each of the 128 pages of pool d once; slot j of that pool owns entries j * 16 to (j + 1) * 16 - 1.
All inputs are finite; a program needn't handle non-finite values.
Results may differ from a plain program's by a relative error of at most 0.0057.
Values may be sent and summed in bfloat16 or wider, within the bound.
A program may use at most 128 MiB of HBM per device.

v0:
```python
import math

import jax
import jax.numpy as jnp
from jax import lax
from jax.sharding import PartitionSpec as P

STATE = 16
CONV = 4
DT_RANK = 512
HQ = 64
KVH = 8
HD = 128
STEPS = 2


def convolve(convs, tokens, conv_weight, conv_bias):
    window = jnp.concatenate([convs, tokens.astype(jnp.float32)], axis=1)
    results = []
    for step in range(STEPS):
        pre = conv_bias + window[:, step] * conv_weight[0]
        for tap in range(1, CONV):
            pre = pre + window[:, step + tap] * conv_weight[tap]
        results.append(jax.nn.silu(pre).astype(jnp.bfloat16))
    return jnp.stack(results, axis=1)


def project(mixed, proj_weight):
    partial_sum = jnp.einsum("rtc,cx->rtx", mixed, proj_weight, preferred_element_type=jnp.float32)
    return lax.psum(partial_sum, ("req", "tp"))


def step_sizes(proj, dt_weight, bias_cols):
    low = proj[:, :, :DT_RANK].astype(jnp.bfloat16)
    return jax.nn.softplus(
        jnp.einsum("rtk,kc->rtc", low, dt_weight, preferred_element_type=jnp.float32) + bias_cols
    )


def advance(hidden, mixed, delta, proj, gates, decay_log, skip_gain):
    rate = -jnp.exp(decay_log)
    results = []
    for step in range(STEPS):
        in_map = proj[:, step, DT_RANK : DT_RANK + STATE]
        out_map = proj[:, step, DT_RANK + STATE :]
        inputf = lax.optimization_barrier(mixed[:, step]).astype(jnp.float32)
        rates_now = delta[:, step]
        hidden = (
            jnp.exp(rates_now[:, None, :] * rate[None]) * hidden
            + rates_now[:, None, :] * in_map[:, :, None] * inputf[:, None, :]
        )
        value = jnp.sum(out_map[:, :, None] * hidden, axis=1) + skip_gain * inputf
        results.append(
            (value * jax.nn.silu(gates[:, step].astype(jnp.float32))).astype(jnp.bfloat16)
        )
    return jnp.stack(results, axis=1)


def attend(query, key_cache, value_cache, fresh, lens, heads, kv_heads):
    rows = query.shape[0]
    group = heads // kv_heads
    scale = 1.0 / math.sqrt(HD)
    queryq = query.reshape(rows, STEPS, kv_heads, group, HD)
    keys = key_cache.reshape(rows, -1, kv_heads, HD)
    values = value_cache.reshape(rows, -1, kv_heads, HD)
    new_keys = fresh[:, :, 0].reshape(rows, STEPS, kv_heads, HD)
    new_values = fresh[:, :, 1].reshape(rows, STEPS, kv_heads, HD)
    old = jnp.einsum("btkgd,bnkd->btkgn", queryq, keys, preferred_element_type=jnp.float32) * scale
    new = (
        jnp.einsum("btkgd,bskd->btkgs", queryq, new_keys, preferred_element_type=jnp.float32)
        * scale
    )
    live = jnp.arange(keys.shape[1])[None, :] < lens[:, None]
    causal = jnp.arange(STEPS)[None, :] <= jnp.arange(STEPS)[:, None]
    old = jnp.where(live[:, None, None, None, :], old, -1e30)
    new = jnp.where(causal[None, :, None, None, :], new, -1e30)
    top = jnp.maximum(jnp.max(old, axis=-1, keepdims=True), jnp.max(new, axis=-1, keepdims=True))
    exp_old = jnp.exp(old - top)
    exp_new = jnp.exp(new - top)
    total = jnp.sum(exp_old, axis=-1, keepdims=True) + jnp.sum(exp_new, axis=-1, keepdims=True)
    w_old = (exp_old / total).astype(jnp.bfloat16)
    w_new = (exp_new / total).astype(jnp.bfloat16)
    out = jnp.einsum("btkgn,bnkd->btkgd", w_old, values, preferred_element_type=jnp.float32)
    out = out + jnp.einsum(
        "btkgs,bskd->btkgd", w_new, new_values, preferred_element_type=jnp.float32
    )
    return out.reshape(rows, STEPS, heads * HD).astype(jnp.bfloat16)


def local(
    ssm_state,
    conv_state,
    token_input,
    gate_input,
    conv_weight,
    conv_bias,
    proj_weight,
    dt_weight,
    dt_bias,
    decay_log,
    skip_gain,
    queries,
    kv_pages,
    new_kv,
    page_table,
    context_len,
    decode_row,
):
    slots = ssm_state.shape[0]
    total = decode_row.shape[0]
    cols = token_input.shape[2]
    source = jnp.zeros((total,), jnp.int32).at[decode_row].set(jnp.arange(total, dtype=jnp.int32))
    offset = lax.axis_index("req") * cols
    heads = HQ // lax.axis_size("tp")
    kv_heads = KVH // lax.axis_size("tp")
    flat_pages = page_table.reshape(-1)
    key_cache = kv_pages[0][flat_pages].reshape(slots, -1, kv_heads * HD)
    value_cache = kv_pages[1][flat_pages].reshape(slots, -1, kv_heads * HD)
    attended = attend(queries, key_cache, value_cache, new_kv, context_len, heads, kv_heads)
    spread = lax.all_to_all(attended, "req", split_axis=2, concat_axis=0, tiled=True)
    attention_out = spread[source]
    bias_cols = lax.dynamic_slice_in_dim(dt_bias, offset, cols, 0)
    tok_slot, gate_slot = (
        lax.all_to_all(token_input[decode_row], "req", split_axis=0, concat_axis=2, tiled=True),
        lax.all_to_all(gate_input[decode_row], "req", split_axis=0, concat_axis=2, tiled=True),
    )
    mixed_slot = convolve(conv_state, tok_slot, conv_weight, conv_bias)
    mixed_cols = lax.all_to_all(mixed_slot, "req", split_axis=2, concat_axis=0, tiled=True)
    proj = project(mixed_cols, proj_weight)
    delta_cols = step_sizes(proj, dt_weight, bias_cols)
    delta = lax.all_to_all(delta_cols, "req", split_axis=0, concat_axis=2, tiled=True)
    mine = lax.dynamic_slice_in_dim(proj, lax.axis_index("req") * slots, slots, 0)
    result = advance(ssm_state, mixed_slot, delta, mine, gate_slot, decay_log, skip_gain)
    back = lax.all_to_all(result, "req", split_axis=2, concat_axis=0, tiled=True)
    mamba_out = back[source]
    return (mamba_out, attention_out)


def solution(mesh):
    in_specs = (
        P(("groups", "req"), None, "tp"),
        P(("groups", "req"), None, "tp"),
        P("groups", None, ("tp", "req")),
        P("groups", None, ("tp", "req")),
        P(None, "tp"),
        P("tp"),
        P(("tp", "req"), None),
        P(None, ("tp", "req")),
        P("tp"),
        P(None, "tp"),
        P("tp"),
        P(("groups", "req"), None, "tp"),
        P(None, ("groups", "req"), None, "tp"),
        P(("groups", "req"), None, None, "tp"),
        P(("groups", "req"), None),
        P(("groups", "req")),
        P("groups"),
    )
    out_specs = (P("groups", None, ("tp", "req")), P("groups", None, ("tp", "req")))
    return jax.shard_map(local, mesh=mesh, in_specs=in_specs, out_specs=out_specs, check_vma=False)
```

profile of v0, /device:TPU:0, one launch (start us, length us, event | category | flops | bytes accessed | tf_op | source)
XLA Modules:
  0.0 266.2 jit_solution(16450474359263013465)
XLA Ops:
  7.2 0.8 compare_select_fusion.3
  7.9 0.5 copy-done.24
  8.5 2.7 %gather_fusion = bf16[64,2,1024]{2,1,0:T(2,128)(2,1)} fusion(bf16[64,2,1024]{2,1,0:T(2,128)(2,1)} %param.19, s32[1024]{0:T(1024)S(1)} %pad_clamp_fusion.2), kind=kCustom, calls=%fused_computation | custom fusion | bytes 524544 | tf_op jit(solution)/shard_map/gather | solution.py:124
  11.2 7.3 %all-to-all-start = ((bf16[64,2,1024]{2,1,0:T(2,128)(2,1)}), bf16[64,2,1024]{2,1,0:T(2,128)(2,1)S(1)}, u32[]{:S(2)}, u32[]{:S(2)}) async-start(bf16[64,2,1024]{2,1,0:T(2,128)(2,1)} %gather_fusion), calls=%async_computation | async-start | bytes 524288 | tf_op jit(solution)/shard_map/all_to_all | solution.py:124
  18.5 2.0 fusion.63
  20.4 1.9 exponential_negate_fusion
  22.4 4.6 %slice_bitcast_fusion.1 = (bf16[128,16,512]{2,1,0:T(8,128)(2,1)}, bf16[128,16,512]{2,1,0:T(8,128)(2,1)}) fusion(bf16[2,128,16,512]{3,2,1,0:T(8,128)(2,1)} %param.29), kind=kLoop, calls=%fused_computation.15 | loop fusion | bytes 8388608 | tf_op jit(solution)/shard_map/squeeze | solution.py:118
  27.1 2.3 gather_fusion.4
  29.3 2.1 reshape_reshape.7
  31.5 1.1 reshape.157
  32.5 0.2 slice_reduce_fusion
  32.7 0.7 fusion.65
  33.5 0.1 iota_compare_fusion
  33.5 3.1 %fusion.64 = (f32[8,2,4,8]{3,1,2,0:T(2,128)S(1)}, f32[8,2,4,8,256]{4,3,1,2,0:T(8,128)}) fusion(bf16[8,2,4,8,128]{4,3,2,1,0:T(8,128)(2,1)S(1)} %reshape.157, bf16[8,256,4,128,1]{3,2,1,0,4:T(4,128)(2,1)} %bitcast.173, pred[8,256]{1,0:T(8,128)(4,1)S(1)} %iota_compare_fusion), kind=kOutput, calls=%fused_computation.109 | convolution fusion | flops 33947136 | bytes 2756608 | tf_op jit(solution)/shard_map/btkgd,bnkd->btkgn/dot_general | solution.py:68
  36.6 0.1 copy.115
  36.7 0.8 copy-done.1
  37.5 0.2 multiply_convert_fusion.3
  37.8 6.7 %copy.116 = bf16[8,2,8192]{0,1,2:T(2,128)(2,1)} copy(bf16[8,2,8192]{2,0,1:T(8,128)(2,1)S(1)} %pad_maximum_fusion) | data formatting | bytes 524288 | tf_op jit(solution)/shard_map/stack | solution.py:25
  44.5 6.4 %reshape.235 = bf16[8,2,8192]{2,1,0:T(2,128)(2,1)} reshape(bf16[8192,2,8]{2,1,0:T(2,128)(2,1)} %bitcast.164) | data formatting | bytes 524288
  50.9 6.0 %all-to-all-start.1 = ((bf16[8,2,8192]{2,1,0:T(2,128)(2,1)}), bf16[8,2,8192]{2,1,0:T(2,128)(2,1)S(1)}, u32[]{:S(2)}, u32[]{:S(2)}) async-start(bf16[8,2,8192]{2,1,0:T(2,128)(2,1)} %reshape.235), calls=%async_computation.1 | async-start | bytes 524288 | tf_op jit(solution)/shard_map/all_to_all | solution.py:128
  56.9 0.7 fusion.55
  57.7 1.8 gather_fusion.1
  59.5 2.4 gather_fusion.3
  61.9 2.1 reshape_reshape.6
  63.9 1.3 fusion.29
  65.3 0.8 add.176
  66.1 0.6 copy-done.20
  66.7 1.8 convolution_bitcast_fusion
  68.5 6.0 %all-to-all-start.3 = ((bf16[64,2,1024]{2,1,0:T(2,128)(2,1)}), bf16[64,2,1024]{2,1,0:T(2,128)(2,1)}, u32[]{:S(2)}, u32[]{:S(2)}) async-start(bf16[64,2,1024]{2,1,0:T(2,128)(2,1)} %gather_fusion.1), calls=%async_computation.3 | async-start | bytes 524288 | tf_op jit(solution)/shard_map/all_to_all | solution.py:125
  74.5 0.0 all-reduce.2.cloned.1.call-start
  74.5 5.9 %reshape.236 = bf16[8192,2,8]{2,1,0:T(2,128)(2,1)} reshape(bf16[8,2,8192]{2,1,0:T(2,128)(2,1)S(1)} %all-to-all-done.1) | data formatting | bytes 524288
  80.5 9.0 %copy.117 = bf16[8,2,8,1024]{3,0,2,1:T(8,128)(2,1)S(1)} copy(bf16[8,2,8,1024]{0,1,3,2:T(2,128)(2,1)} %bitcast.165) | data formatting | bytes 524288 | tf_op jit(solution)/shard_map/all_to_all | solution.py:128
  89.5 1.3 fusion.24
  90.8 0.0 all-reduce.2.cloned.1.call-update
  90.8 1.6 fusion.19
  92.4 1.2 copy.152
  93.6 2.8 %reshape.239 = bf16[8,2,4096]{2,1,0:T(2,128)(2,1)} reshape(bf16[4096,2,8]{2,1,0:T(2,128)(2,1)S(1)} %bitcast.168) | data formatting | bytes 262144
  96.4 0.8 dynamic_slice.7
  97.2 83.6 %all-reduce.2.cloned.1.call-done = f32[64,2,544]{2,0,1:T(8,128)} async-done(((f32[64,2,544]{2,0,1:T(8,128)}), f32[64,2,544]{2,0,1:T(8,128)}) %all-reduce.2.cloned.1.call-update) | async-done | bytes 278544 | tf_op jit(solution)/shard_map/psum | solution.py:30
  180.8 1.8 compare_select_fusion
  182.6 1.2 copy.118
  183.8 5.6 %all-to-all-start.2 = ((f32[64,2,1024]{2,1,0:T(2,128)}), f32[64,2,1024]{2,1,0:T(2,128)S(1)}, u32[]{:S(2)}, u32[]{:S(2)}) async-start(f32[64,2,1024]{2,1,0:T(2,128)} %copy.118), calls=%async_computation.2 | async-start | bytes 1048576 | tf_op jit(solution)/shard_map/all_to_all | solution.py:131
  189.4 1.0 multiply_convert_fusion
  190.5 0.8 convert_element_type.68
  191.3 0.7 convert_element_type.73
  192.0 1.7 copy.120
  193.7 0.8 dynamic-slice_bitcast_fusion.1
  194.5 8.6 %all-to-all-done.2 = f32[64,2,1024]{2,1,0:T(2,128)S(1)} async-done(((f32[64,2,1024]{2,1,0:T(2,128)}), f32[64,2,1024]{2,1,0:T(2,128)S(1)}, u32[]{:S(2)}, u32[]{:S(2)}) %all-to-all-start.2) | async-done | bytes 524320 | tf_op jit(solution)/shard_map/all_to_all | solution.py:131
  203.1 4.2 %all-to-all-start.5 = ((bf16[8,2,4096]{2,1,0:T(2,128)(2,1)}), bf16[8,2,4096]{2,1,0:T(2,128)(2,1)}, u32[]{:S(2)}, u32[]{:S(2)}) async-start(bf16[8,2,4096]{2,1,0:T(2,128)(2,1)} %reshape.239), calls=%async_computation.5 | async-start | bytes 262144 | tf_op jit(solution)/shard_map/all_to_all | solution.py:120
  207.3 0.3 copy.189
  207.7 0.1 all_to_all.80
  207.8 5.2 %multiply_reduce_fusion.1 = (f32[8,8192]{1,0:T(8,128)S(1)}, f32[8,8192]{1,0:T(8,128)S(1)}) fusion(f32[8,16,8192]{2,1,0:T(8,128)} %param.17, f32[8,8192]{1,0:T(8,128)} %convert_element_type.68, f32[8,16]{1,0:T(8,128)S(1)} %get-tuple-element.15, f32[16,8192]{1,0:T(8,128)S(1)} %copy-done.5, f32[8,8192]{1,0:T(8,128)S(1)} %get-tuple-element.13, ...), kind=kLoop, calls=%fused_computation.8 | loop fusion | flops 14548992 | bytes 6293504 | tf_op jit(solution)/shard_map/reduce_sum | solution.py:52
  213.1 0.2 fusion.51
  213.3 6.7 %copy.121 = bf16[8,2,8192]{0,1,2:T(2,128)(2,1)} copy(bf16[8,2,8192]{2,0,1:T(8,128)(2,1)S(1)} %pad_maximum_fusion.1) | data formatting | bytes 524288 | tf_op jit(solution)/shard_map/stack | solution.py:56
  220.1 6.4 %reshape.237 = bf16[8,2,8192]{2,1,0:T(2,128)(2,1)} reshape(bf16[8192,2,8]{2,1,0:T(2,128)(2,1)} %bitcast.166) | data formatting | bytes 524288
  226.5 5.7 %all-to-all-start.4 = ((bf16[8,2,8192]{2,1,0:T(2,128)(2,1)}), bf16[8,2,8192]{2,1,0:T(2,128)(2,1)S(1)}, u32[]{:S(2)}, u32[]{:S(2)}) async-start(bf16[8,2,8192]{2,1,0:T(2,128)(2,1)} %reshape.237), calls=%async_computation.4 | async-start | bytes 524288 | tf_op jit(solution)/shard_map/all_to_all | solution.py:134
  232.2 0.9 scatter_custom_fusion
  233.1 3.3 %reshape.240 = bf16[4096,2,8]{2,1,0:T(2,128)(2,1)S(1)} reshape(bf16[8,2,4096]{2,1,0:T(2,128)(2,1)} %all-to-all-done.5) | data formatting | bytes 262144
  236.4 3.2 %copy.154 = bf16[8,2,8,512]{3,0,2,1:T(8,128)(2,1)} copy(bf16[8,2,8,512]{0,1,3,2:T(2,128)(2,1)S(1)} %bitcast.169) | data formatting | bytes 262144 | tf_op jit(solution)/shard_map/all_to_all | solution.py:120
  239.6 1.0 copy.135
  240.7 1.5 gather_fusion.5
  242.2 5.9 %reshape.238 = bf16[8192,2,8]{2,1,0:T(2,128)(2,1)} reshape(bf16[8,2,8192]{2,1,0:T(2,128)(2,1)S(1)} %all-to-all-done.4) | data formatting | bytes 524288
  248.1 9.5 %copy.122 = bf16[8,2,8,1024]{3,1,0,2:T(2,128)(2,1)S(1)} copy(bf16[8,2,8,1024]{0,1,3,2:T(2,128)(2,1)} %bitcast.167) | data formatting | bytes 524288 | tf_op jit(solution)/shard_map/all_to_all | solution.py:134
  257.6 1.8 gather_fusion.2
  (67 shorter events, 0.3 us)
Async XLA Ops:
  7.2 82.3 %copy-start = (bf16[1024,544]{0,1:T(8,128)(2,1)S(1)}, bf16[1024,544]{0,1:T(8,128)(2,1)}, u32[]{:S(2)}) copy-start(bf16[1024,544]{0,1:T(8,128)(2,1)} %param.23) | copy-start | bytes 3342340
  7.9 0.5 copy-start.24
  11.2 25.4 %all-to-all-start = ((bf16[64,2,1024]{2,1,0:T(2,128)(2,1)}), bf16[64,2,1024]{2,1,0:T(2,128)(2,1)S(1)}, u32[]{:S(2)}, u32[]{:S(2)}) async-start(bf16[64,2,1024]{2,1,0:T(2,128)(2,1)} %gather_fusion), calls=%async_computation | async-start | bytes 524288 | tf_op jit(solution)/shard_map/all_to_all | solution.py:124
  22.4 4.6 %copy-start.25 = (s32[1,128]{1,0:T(1,128)S(1)}, s32[1,128]{1,0:T(1,128)}, u32[]{:S(2)}) copy-start(s32[1,128]{1,0:T(1,128)} %param.31) | copy-start | bytes 1540
  27.0 4.4 %copy-start.22 = (s32[1024]{0:T(1024)}, s32[1024]{0:T(1024)S(1)}, u32[]{:S(2)}) copy-start(s32[1024]{0:T(1024)S(1)} %pad_clamp_fusion) | copy-start | bytes 12292
  27.0 5.5 %copy-start.18 = (bf16[8,2,2,512]{3,2,1,0:T(2,128)(2,1)S(1)}, bf16[8,2,2,512]{3,2,1,0:T(2,128)(2,1)}, u32[]{:S(2)}) copy-start(bf16[8,2,2,512]{3,2,1,0:T(2,128)(2,1)} %param.30) | copy-start | bytes 98308
  27.0 6.4 %copy-start.23 = (s32[8]{0:T(128)S(1)}, s32[8]{0:T(128)}, u32[]{:S(2)}) copy-start(s32[8]{0:T(128)} %param.32) | copy-start | bytes 100
  31.4 6.1 %copy-start.3 = (f32[8,3,8192]{2,0,1:T(8,128)S(1)}, f32[8,3,8192]{2,0,1:T(8,128)}, u32[]{:S(2)}) copy-start(f32[8,3,8192]{2,0,1:T(8,128)} %param.18) | copy-start | bytes 2359300
  31.4 6.1 %copy-start.12 = (f32[1,8192]{1,0:T(1,128)S(1)}, f32[1,8192]{1,0:T(1,128)}, u32[]{:S(2)}) copy-start(f32[1,8192]{1,0:T(1,128)} %get-tuple-element.21) | copy-start | bytes 98308
  31.4 6.1 %copy-start.14 = (f32[1,8192]{1,0:T(1,128)S(1)}, f32[1,8192]{1,0:T(1,128)}, u32[]{:S(2)}) copy-start(f32[1,8192]{1,0:T(1,128)} %get-tuple-element.22) | copy-start | bytes 98308
  31.4 6.1 %copy-start.15 = (f32[1,8192]{1,0:T(1,128)S(1)}, f32[1,8192]{1,0:T(1,128)}, u32[]{:S(2)}) copy-start(f32[1,8192]{1,0:T(1,128)} %get-tuple-element.23) | copy-start | bytes 98308
  31.4 6.1 %copy-start.17 = (f32[8192]{0:T(1024)S(1)}, f32[8192]{0:T(1024)}, u32[]{:S(2)}) copy-start(f32[8192]{0:T(1024)} %param.22) | copy-start | bytes 98308
  33.5 23.5 %copy-start.19 = (f32[8,2,4,8,2]{3,4,1,2,0:T(2,128)}, f32[8,2,4,8,2]{3,4,1,2,0:T(2,128)S(1)}, u32[]{:S(2)}) copy-start(f32[8,2,4,8,2]{3,4,1,2,0:T(2,128)S(1)} %get-tuple-element.27) | copy-start | bytes 12292
  36.7 0.8 copy-start.1
  37.8 19.9 %copy-start.16 = (bf16[64,2,1024]{2,1,0:T(2,128)(2,1)S(1)}, bf16[64,2,1024]{2,1,0:T(2,128)(2,1)}, u32[]{:S(2)}) copy-start(bf16[64,2,1024]{2,1,0:T(2,128)(2,1)} %param.20) | copy-start | bytes 786436
  50.9 17.6 %all-to-all-start.1 = ((bf16[8,2,8192]{2,1,0:T(2,128)(2,1)}), bf16[8,2,8192]{2,1,0:T(2,128)(2,1)S(1)}, u32[]{:S(2)}, u32[]{:S(2)}) async-start(bf16[8,2,8192]{2,1,0:T(2,128)(2,1)} %reshape.235), calls=%async_computation.1 | async-start | bytes 524288 | tf_op jit(solution)/shard_map/all_to_all | solution.py:128
  66.1 0.6 copy-start.20
  68.5 115.3 %all-to-all-start.3 = ((bf16[64,2,1024]{2,1,0:T(2,128)(2,1)}), bf16[64,2,1024]{2,1,0:T(2,128)(2,1)}, u32[]{:S(2)}, u32[]{:S(2)}) async-start(bf16[64,2,1024]{2,1,0:T(2,128)(2,1)} %gather_fusion.1), calls=%async_computation.3 | async-start | bytes 524288 | tf_op jit(solution)/shard_map/all_to_all | solution.py:125
  74.5 106.3 %all-reduce.2.cloned.1.call-start = ((), (), s32[]{:S(2)}) async-start(), calls=%async_computation.6 | async-start | bytes 655360 | tf_op jit(solution)/shard_map/psum | solution.py:30
  80.5 10.3 %copy-start.6 = (bf16[8,256,4,128]{3,2,1,0:T(4,128)(2,1)S(1)}, bf16[8,256,4,128]{3,2,1,0:T(4,128)(2,1)}, u32[]{:S(2)}) copy-start(bf16[8,256,4,128]{3,2,1,0:T(4,128)(2,1)} %reshape_reshape.6) | copy-start | bytes 6291460
  92.4 97.0 %copy-start.13 = (f32[1,8192]{1,0:T(1,128)S(1)}, f32[1,8192]{1,0:T(1,128)}, u32[]{:S(2)}) copy-start(f32[1,8192]{1,0:T(1,128)} %get-tuple-element.21) | copy-start | bytes 98308
  96.4 93.0 %copy-start.2 = (f32[8,8,2,1024]{3,1,0,2:T(8,128)S(1)}, f32[8,8,2,1024]{3,1,0,2:T(8,128)}, u32[]{:S(2)}) copy-start(f32[8,8,2,1024]{3,1,0,2:T(8,128)} %copy-done.1) | copy-start | bytes 1572868
  96.4 93.0 %copy-start.4 = (f32[8,3,8192]{2,0,1:T(8,128)S(1)}, f32[8,3,8192]{2,0,1:T(8,128)}, u32[]{:S(2)}) copy-start(f32[8,3,8192]{2,0,1:T(8,128)} %param.18) | copy-start | bytes 2359300
  182.6 25.2 %copy-start.5 = (f32[16,8192]{1,0:T(8,128)S(1)}, f32[16,8192]{1,0:T(8,128)}, u32[]{:S(2)}) copy-start(f32[16,8192]{1,0:T(8,128)} %exponential_negate_fusion) | copy-start | bytes 1572868
  183.8 19.3 %all-to-all-start.2 = ((f32[64,2,1024]{2,1,0:T(2,128)}), f32[64,2,1024]{2,1,0:T(2,128)S(1)}, u32[]{:S(2)}, u32[]{:S(2)}) async-start(f32[64,2,1024]{2,1,0:T(2,128)} %copy.118), calls=%async_computation.2 | async-start | bytes 1048576 | tf_op jit(solution)/shard_map/all_to_all | solution.py:131
  190.5 3.2 %copy-start.7 = (bf16[8,8192]{1,0:T(8,128)(2,1)}, bf16[8,8192]{1,0:T(8,128)(2,1)S(1)}, u32[]{:S(2)}) copy-start(bf16[8,8192]{1,0:T(8,128)(2,1)S(1)} %get-tuple-element.8) | copy-start | bytes 393220
  190.5 3.2 %copy-start.9 = (bf16[8,8192]{1,0:T(8,128)(2,1)}, bf16[8,8192]{1,0:T(8,128)(2,1)S(1)}, u32[]{:S(2)}) copy-start(bf16[8,8192]{1,0:T(8,128)(2,1)S(1)} %get-tuple-element.9) | copy-start | bytes 393220
  203.1 23.3 %all-to-all-start.5 = ((bf16[8,2,4096]{2,1,0:T(2,128)(2,1)}), bf16[8,2,4096]{2,1,0:T(2,128)(2,1)}, u32[]{:S(2)}, u32[]{:S(2)}) async-start(bf16[8,2,4096]{2,1,0:T(2,128)(2,1)} %reshape.239), calls=%async_computation.5 | async-start | bytes 262144 | tf_op jit(solution)/shard_map/all_to_all | solution.py:120
  207.6 5.4 %copy-start.8 = (bf16[8,8192]{1,0:T(8,128)(2,1)S(1)}, bf16[8,8192]{1,0:T(8,128)(2,1)}, u32[]{:S(2)}) copy-start(bf16[8,8192]{1,0:T(8,128)(2,1)} %copy-done.7) | copy-start | bytes 393220
  207.6 5.4 %copy-start.10 = (bf16[8,8192]{1,0:T(8,128)(2,1)S(1)}, bf16[8,8192]{1,0:T(8,128)(2,1)}, u32[]{:S(2)}) copy-start(bf16[8,8192]{1,0:T(8,128)(2,1)} %copy-done.9) | copy-start | bytes 393220
  207.7 5.4 %copy-start.11 = (bf16[8,8,2,1024]{3,1,0,2:T(8,128)(2,1)S(1)}, bf16[8,8,2,1024]{3,1,0,2:T(8,128)(2,1)}, u32[]{:S(2)}) copy-start(bf16[8,8,2,1024]{3,1,0,2:T(8,128)(2,1)} %copy.120) | copy-start | bytes 786436
  207.7 5.4 %copy-start.21 = (f32[8192]{0:T(1024)S(1)}, f32[8192]{0:T(1024)}, u32[]{:S(2)}) copy-start(f32[8192]{0:T(1024)} %param.27) | copy-start | bytes 98308
  226.5 15.7 %all-to-all-start.4 = ((bf16[8,2,8192]{2,1,0:T(2,128)(2,1)}), bf16[8,2,8192]{2,1,0:T(2,128)(2,1)S(1)}, u32[]{:S(2)}, u32[]{:S(2)}) async-start(bf16[8,2,8192]{2,1,0:T(2,128)(2,1)} %reshape.237), calls=%async_computation.4 | async-start | bytes 524288 | tf_op jit(solution)/shard_map/all_to_all | solution.py:134
Sparse Core Ops, SparseCore 0:
  90.9 89.8 all-reduce.1
where the time goes:
time: 268 us; the launch traced here: 266 us
  local copies, waits for them, and re-layouts  101 us (38%)
  waiting for transfers between devices  92.2 us (34%)
  starting transfers between devices  34.8 us (13%)
  between operations  14.5 us (5%)
  other arithmetic  13.9 us (5%)
  matrix products  10.2 us (4%)
    psum x1, waiting for transfers between devices, project(): return lax.psum(partial_sum, ('req', 'tp'))  83.6 us
    unnamed x58, local copies, waits for them, and re-layouts  32.8 us
    all_to_all x1, local copies, waits for them, and re-layouts, local(): lax.all_to_all(result, 'req', split_axis=2, concat_axis=0, tiled=True)  9.49 us
    all_to_all x1, local copies, waits for them, and re-layouts, local(): lax.all_to_all(mixed_slot, 'req', split_axis=2, concat_axis=0, tiled=True)  9.03 us
    all_to_all x1, waiting for transfers between devices, local(): lax.all_to_all(delta_cols, 'req', split_axis=0, concat_axis=2, tiled=True)  8.61 us
    all_to_all x1, starting transfers between devices, local(): lax.all_to_all(token_input[decode_row], 'req', split_axis=0, concat_axis=...  7.28 us
    another operation x1, local copies, waits for them, and re-layouts, advance(): return jnp.stack(results, axis=1)  6.72 us
    another operation x1, local copies, waits for them, and re-layouts, convolve(): return jnp.stack(results, axis=1)  6.72 us
  transfers between devices with their start and end apart: 7, of which 2 were waited for; matrix products, arithmetic and copies ran while one was open for 33% of the time, Pallas kernels for 0%

commit v1 on v0

--- a/solution.py
+++ b/solution.py
@@ -1,8 +1,11 @@
+import functools
 import math
 
 import jax
 import jax.numpy as jnp
 from jax import lax
+from jax.experimental import pallas as pl
+from jax.experimental.pallas import tpu as pltpu
 from jax.sharding import PartitionSpec as P
 
 STATE = 16
@@ -136,6 +139,459 @@
     return (mamba_out, attention_out)
 
 
+ROWS = 16
+
+
+def block_kernel(
+    n,
+    slots,
+    cols,
+    acols,
+    kv_heads,
+    pre_ref,
+    tok_ref,
+    gate_ref,
+    vec_ref,
+    perm_col_ref,
+    perm_row_ref,
+    query_ref,
+    fresh_ref,
+    bias_ref,
+    fresh_bias_ref,
+    state_hbm,
+    kv_hbm,
+    pw_hbm,
+    dtw_hbm,
+    decay_hbm,
+    mamba_ref,
+    att_ref,
+    state,
+    kv,
+    pw,
+    dtw,
+    decay,
+    pre_send,
+    pre_recv,
+    tok_send,
+    tok_recv,
+    part_send,
+    part_recv,
+    low_send,
+    low_recv,
+    del_send,
+    del_recv,
+    val_send,
+    val_recv,
+    att_send,
+    att_recv,
+    zbuf,
+    vbuf,
+    maps_t,
+    load_sem,
+    pre_ss,
+    pre_rs,
+    tok_ss,
+    tok_rs,
+    part_ss,
+    part_rs,
+    low_ss,
+    low_rs,
+    del_ss,
+    del_rs,
+    val_ss,
+    val_rs,
+    att_ss,
+    att_rs,
+):
+    me = lax.axis_index("req")
+    core = lax.axis_index("tp")
+    total = 2 * n
+    flat = core * n + me
+    rows = n * ROWS
+    f32, bf16 = jnp.float32, jnp.bfloat16
+
+    loads = [
+        pltpu.make_async_copy(src, dst, load_sem.at[i])
+        for i, (src, dst) in enumerate(
+            ((kv_hbm, kv), (pw_hbm, pw), (dtw_hbm, dtw), (state_hbm, state), (decay_hbm, decay))
+        )
+    ]
+    for load in loads:
+        load.start()
+
+    barrier = pltpu.get_barrier_semaphore()
+
+    @pl.loop(1, total)
+    def _(k):
+        other = lax.rem(flat + k, total)
+        pl.semaphore_signal(
+            barrier,
+            inc=1,
+            device_id={"req": lax.rem(other, n), "tp": other // n},
+            device_id_type=pl.DeviceIdType.MESH,
+        )
+
+    def req_copy(src, dst, ss, rs, peer, slot):
+        return pltpu.make_async_remote_copy(
+            src_ref=src.at[peer],
+            dst_ref=dst.at[slot],
+            send_sem=ss.at[peer],
+            recv_sem=rs.at[slot],
+            device_id={"req": peer, "tp": core},
+            device_id_type=pl.DeviceIdType.MESH,
+        )
+
+    def req_start(src, dst, ss, rs):
+        @pl.loop(1, n)
+        def _(k):
+            peer = lax.rem(me + k, n)
+            req_copy(src, dst, ss, rs, peer, me).start()
+
+    def req_wait(src, dst, ss, rs):
+        @pl.loop(1, n)
+        def _(k):
+            peer = lax.rem(me + k, n)
+            req_copy(src, dst, ss, rs, peer, peer).wait_recv()
+
+    def req_drain(src, dst, ss, rs):
+        @pl.loop(1, n)
+        def _(k):
+            peer = lax.rem(me + k, n)
+            req_copy(src, dst, ss, rs, peer, me).wait_send()
+
+    def all_copy(src, dst, ss, rs, peer, slot):
+        return pltpu.make_async_remote_copy(
+            src_ref=src,
+            dst_ref=dst.at[slot],
+            send_sem=ss.at[peer],
+            recv_sem=rs.at[slot],
+            device_id={"req": lax.rem(peer, n), "tp": peer // n},
+            device_id_type=pl.DeviceIdType.MESH,
+        )
+
+    for j in range(n):
+        pre_send[j] = pre_ref[:, j * cols : (j + 1) * cols].astype(bf16)
+    lane = lax.broadcasted_iota(jnp.int32, (rows, rows), 1)
+    perm = jnp.where(perm_col_ref[...] == lane, 1.0, 0.0).astype(bf16)
+    tok = jnp.dot(perm, tok_ref[...], preferred_element_type=f32)
+    tok_send[...] = tok.astype(bf16).reshape(n, ROWS, cols)
+
+    pl.semaphore_wait(barrier, total - 1)
+    req_start(pre_send, pre_recv, pre_ss, pre_rs)
+    req_start(tok_send, tok_recv, tok_ss, tok_rs)
+    pre_recv[pl.ds(me, 1)] = pre_send[pl.ds(me, 1)]
+    tok_recv[pl.ds(me, 1)] = tok_send[pl.ds(me, 1)]
+
+    loads[0].wait()
+    group = (acols * n) // (kv_heads * HD)
+    per_block = acols // HD
+    scale = 1.0 / math.sqrt(HD)
+    contract = (((1,), (1,)), ((), ()))
+
+    @pl.loop(0, kv_heads)
+    def _(h):
+        lanes = pl.ds(pl.multiple_of(h * HD, HD), HD)
+        q = jnp.concatenate(
+            [
+                query_ref[:, pl.ds(pl.multiple_of((h * group + g) * HD, HD), HD)]
+                for g in range(group)
+            ],
+            axis=0,
+        )
+        old = lax.dot_general(q, kv[0, :, lanes], contract, preferred_element_type=f32)
+        new = lax.dot_general(
+            q, fresh_ref[0, :, lanes], contract, preferred_element_type=f32
+        )
+        old = old.reshape(group, ROWS, -1) * scale + bias_ref[...][None]
+        new = new.reshape(group, ROWS, -1) * scale + fresh_bias_ref[...][None]
+        top = jnp.maximum(
+            jnp.max(old, axis=-1, keepdims=True), jnp.max(new, axis=-1, keepdims=True)
+        )
+        old = jnp.exp(old - top)
+        new = jnp.exp(new - top)
+        norm = jnp.sum(old, axis=-1, keepdims=True) + jnp.sum(new, axis=-1, keepdims=True)
+        old = old.astype(bf16).reshape(group * ROWS, -1)
+        new = new.astype(bf16).reshape(group * ROWS, -1)
+        out = jnp.dot(old, kv[1, :, lanes], preferred_element_type=f32)
+        out = out + jnp.dot(new, fresh_ref[1, :, lanes], preferred_element_type=f32)
+        out = (out.reshape(group, ROWS, HD) / norm).astype(bf16)
+        for g in range(group):
+            place = g % per_block
+            att_send[h * (group // per_block) + g // per_block, :, place * HD : (place + 1) * HD] = out[g]
+
+    here = pl.ds(pl.multiple_of(me * cols, cols), cols)
+    taps = vec_ref[0:2, here]
+    bias_cols = vec_ref[2:3, here]
+    tok4 = tok.reshape(n, 2, 8, cols)
+    req_wait(pre_send, pre_recv, pre_ss, pre_rs)
+    pre4 = pre_recv[...].astype(f32).reshape(n, 2, 8, cols)
+    first = pre4[:, 0] + tok4[:, 0] * taps[1:2][None]
+    second = pre4[:, 1] + tok4[:, 0] * taps[0:1][None] + tok4[:, 1] * taps[1:2][None]
+    mixed = jnp.stack([jax.nn.silu(first), jax.nn.silu(second)], axis=1)
+    mixed = mixed.reshape(rows, cols).astype(bf16)
+    loads[1].wait()
+    part = jnp.dot(mixed, pw[...], preferred_element_type=f32)
+    half = DT_RANK // 2
+    maps = jnp.concatenate(
+        [part[:, DT_RANK:], jnp.zeros((rows, 128 - 2 * STATE), f32)], axis=1
+    )
+    for c in range(2):
+        part_send[c * n : (c + 1) * n, :, :half] = (
+            part[:, c * half : (c + 1) * half].astype(bf16).reshape(n, ROWS, half)
+        )
+        part_send[c * n : (c + 1) * n, :, half:] = maps.astype(bf16).reshape(n, ROWS, 128)
+
+    @pl.loop(1, total)
+    def _(k):
+        peer = lax.rem(flat + k, total)
+        all_copy(part_send.at[peer], part_recv, part_ss, part_rs, peer, flat).start()
+
+    part_recv[pl.ds(flat, 1)] = part_send[pl.ds(flat, 1)]
+
+    @pl.loop(1, total)
+    def _(k):
+        peer = lax.rem(flat + k, total)
+        all_copy(part_send.at[peer], part_recv, part_ss, part_rs, peer, peer).wait_recv()
+
+    summed = jnp.sum(part_recv[...].astype(f32), axis=0)
+    low_send[...] = summed[:, :half].astype(bf16)
+
+    @pl.loop(1, total)
+    def _(k):
+        peer = lax.rem(flat + k, total)
+        all_copy(low_send, low_recv, low_ss, low_rs, peer, flat).start()
+
+    low_recv[pl.ds(flat, 1)] = low_send[...][None]
+    req_start(att_send, att_recv, att_ss, att_rs)
+    att_recv[pl.ds(me, 1)] = att_send[pl.ds(me, 1)]
+    square = jnp.concatenate(
+        [summed[:, half:], jnp.zeros((128 - ROWS, 128), f32)], axis=0
+    )
+    maps_t[...] = jnp.transpose(square)[: 2 * STATE]
+    loads[2].wait()
+
+    @pl.loop(1, total)
+    def _(k):
+        peer = lax.rem(flat + k, total)
+        all_copy(low_send, low_recv, low_ss, low_rs, peer, peer).wait_recv()
+
+    z = jnp.dot(low_recv[:n].reshape(rows, half), dtw[:half], preferred_element_type=f32)
+    z = z + jnp.dot(low_recv[n:].reshape(rows, half), dtw[half:], preferred_element_type=f32)
+    zbuf[...] = (z + bias_cols).reshape(n, ROWS, cols)
+
+    @pl.loop(0, n)
+    def _(k):
+        peer = lax.rem(me + 1 + k, n)
+        block = zbuf[pl.ds(peer, 1)]
+        delta = jnp.maximum(block, 0.0) + jnp.log1p(jnp.exp(-jnp.abs(block)))
+        del_send[pl.ds(peer, 1)] = delta.astype(bf16)
+
+        @pl.when(k < n - 1)
+        def _():
+            req_copy(del_send, del_recv, del_ss, del_rs, peer, me).start()
+
+    del_recv[pl.ds(me, 1)] = del_send[pl.ds(me, 1)]
+    loads[3].wait()
+    loads[4].wait()
+    req_wait(tok_send, tok_recv, tok_ss, tok_rs)
+
+    @pl.loop(0, n)
+    def _(k):
+        peer = lax.rem(me - k + n, n)
+
+        @pl.when(k > 0)
+        def _():
+            req_copy(del_send, del_recv, del_ss, del_rs, peer, peer).wait_recv()
+
+        block = pl.ds(pl.multiple_of(peer * cols, cols), cols)
+        delta = del_recv[peer].astype(f32)
+        toks = tok_recv[peer].astype(f32)
+        w2 = vec_ref[0:1, block]
+        w3 = vec_ref[1:2, block]
+        skip = vec_ref[3:4, block]
+        x0 = pre_ref[0:8, block] + toks[0:8] * w3
+        x1 = pre_ref[8:16, block] + toks[0:8] * w2 + toks[8:16] * w3
+        x = jnp.concatenate([jax.nn.silu(x0), jax.nn.silu(x1)], axis=0)
+        x = x.astype(bf16).astype(f32)
+        dx = delta * x
+        rate = -jnp.exp(decay[:, block])
+        for s in range(slots):
+            h = state[s, :, block]
+            for t in range(STEPS):
+                i = t * slots + s
+                h = jnp.exp(delta[i : i + 1] * rate) * h + dx[i : i + 1] * maps_t[:STATE, i : i + 1]
+                vbuf[i : i + 1, :] = jnp.sum(
+                    h * maps_t[STATE:, i : i + 1], axis=0, keepdims=True
+                )
+        val_send[peer] = (vbuf[...] + skip * x).astype(bf16)
+
+        @pl.when(k > 0)
+        def _():
+            req_copy(val_send, val_recv, val_ss, val_rs, peer, me).start()
+
+    val_recv[pl.ds(me, 1)] = val_send[pl.ds(me, 1)]
+
+    sub = lax.broadcasted_iota(jnp.int32, (rows, rows), 0)
+    back = jnp.where(perm_row_ref[...] == sub, 1.0, 0.0).astype(bf16)
+    gate = jax.nn.silu(gate_ref[...].astype(f32))
+    req_wait(att_send, att_recv, att_ss, att_rs)
+    att = jnp.dot(back, att_recv[...].reshape(rows, acols), preferred_element_type=f32)
+    att_ref[...] = att.astype(bf16)
+    req_wait(val_send, val_recv, val_ss, val_rs)
+    val = jnp.dot(back, val_recv[...].reshape(rows, cols), preferred_element_type=f32)
+    mamba_ref[...] = (val * gate).astype(bf16)
+
+    req_drain(pre_send, pre_recv, pre_ss, pre_rs)
+    req_drain(tok_send, tok_recv, tok_ss, tok_rs)
+    req_drain(att_send, att_recv, att_ss, att_rs)
+    req_drain(del_send, del_recv, del_ss, del_rs)
+    req_drain(val_send, val_recv, val_ss, val_rs)
+
+    @pl.loop(1, total)
+    def _(k):
+        peer = lax.rem(flat + k, total)
+        all_copy(part_send.at[peer], part_recv, part_ss, part_rs, peer, flat).wait_send()
+        all_copy(low_send, low_recv, low_ss, low_rs, peer, flat).wait_send()
+
+
+def local_kernel(
+    ssm_state,
+    conv_state,
+    token_input,
+    gate_input,
+    conv_weight,
+    conv_bias,
+    proj_weight,
+    dt_weight,
+    dt_bias,
+    decay_log,
+    skip_gain,
+    queries,
+    kv_pages,
+    new_kv,
+    page_table,
+    context_len,
+    decode_row,
+):
+    n = lax.axis_size("req")
+    slots = ssm_state.shape[0]
+    width = ssm_state.shape[2]
+    total = decode_row.shape[0]
+    cols = token_input.shape[2]
+    acols = queries.shape[2] // n
+    kv_heads = KVH // lax.axis_size("tp")
+    pages, page = kv_pages.shape[1:3]
+    per_slot = pages // slots
+    rows = total * STEPS
+    pre0 = (
+        conv_bias
+        + conv_state[:, 0] * conv_weight[0]
+        + conv_state[:, 1] * conv_weight[1]
+        + conv_state[:, 2] * conv_weight[2]
+    )
+    pre1 = conv_bias + conv_state[:, 1] * conv_weight[0] + conv_state[:, 2] * conv_weight[1]
+    pre = jnp.concatenate([pre0, pre1], axis=0)
+    vecs = jnp.concatenate([conv_weight[2:4], dt_bias[None], skip_gain[None]], axis=0)
+    target = (
+        decode_row.reshape(n, 1, slots) * STEPS + jnp.arange(STEPS, dtype=jnp.int32)[None, :, None]
+    ).reshape(rows)
+    entry = jnp.sum(
+        jnp.where(
+            page_table.reshape(-1, 1) == jnp.arange(pages)[None],
+            jnp.arange(pages, dtype=jnp.int32)[:, None],
+            0,
+        ),
+        axis=0,
+    )
+    place = (entry % per_slot)[:, None] * page + jnp.arange(page)[None]
+    limit = jnp.where(
+        (entry // per_slot)[None] == jnp.arange(slots)[:, None], context_len[:, None], 0
+    )
+    live = (place[None] < limit[:, :, None]).reshape(slots, pages * page)
+    bias = jnp.where(live, 0.0, -1e30).astype(jnp.float32)
+    bias = jnp.concatenate([bias] * STEPS, axis=0)
+    index = jnp.arange(STEPS * slots)
+    own = (index % slots)[:, None] == (index % slots)[None]
+    causal = (index // slots)[None] <= (index // slots)[:, None]
+    fresh_bias = jnp.where(own & causal, 0.0, -1e30).astype(jnp.float32)
+    query_rows = queries.transpose(1, 0, 2).reshape(STEPS * slots, -1)
+    fresh = new_kv.transpose(2, 1, 0, 3).reshape(2, STEPS * slots, -1)
+    kv = kv_pages.reshape(2, pages * page, -1)
+    half = DT_RANK // 2
+    bf16, f32 = jnp.bfloat16, jnp.float32
+    vmem = pl.BlockSpec(memory_space=pltpu.VMEM)
+    hbm = pl.BlockSpec(memory_space=pl.ANY)
+    dma = pltpu.SemaphoreType.DMA
+    mamba, attended = pl.pallas_call(
+        functools.partial(block_kernel, n, slots, cols, acols, kv_heads),
+        out_shape=(
+            jax.ShapeDtypeStruct((rows, cols), bf16),
+            jax.ShapeDtypeStruct((rows, acols), bf16),
+        ),
+        in_specs=[vmem] * 10 + [hbm] * 5,
+        out_specs=(vmem, vmem),
+        scratch_shapes=[
+            pltpu.VMEM(ssm_state.shape, f32),
+            pltpu.VMEM(kv.shape, bf16),
+            pltpu.VMEM(proj_weight.shape, bf16),
+            pltpu.VMEM(dt_weight.shape, bf16),
+            pltpu.VMEM(decay_log.shape, f32),
+            pltpu.VMEM((n, ROWS, cols), bf16),
+            pltpu.VMEM((n, ROWS, cols), bf16),
+            pltpu.VMEM((n, ROWS, cols), bf16),
+            pltpu.VMEM((n, ROWS, cols), bf16),
+            pltpu.VMEM((2 * n, ROWS, half + 128), bf16),
+            pltpu.VMEM((2 * n, ROWS, half + 128), bf16),
+            pltpu.VMEM((ROWS, half), bf16),
+            pltpu.VMEM((2 * n, ROWS, half), bf16),
+            pltpu.VMEM((n, ROWS, cols), bf16),
+            pltpu.VMEM((n, ROWS, cols), bf16),
+            pltpu.VMEM((n, ROWS, cols), bf16),
+            pltpu.VMEM((n, ROWS, cols), bf16),
+            pltpu.VMEM((n, ROWS, acols), bf16),
+            pltpu.VMEM((n, ROWS, acols), bf16),
+            pltpu.VMEM((n, ROWS, cols), f32),
+            pltpu.VMEM((ROWS, cols), f32),
+            pltpu.VMEM((2 * STATE, 128), f32),
+            dma((5,)),
+            dma((n,)),
+            dma((n,)),
+            dma((n,)),
+            dma((n,)),
+            dma((2 * n,)),
+            dma((2 * n,)),
+            dma((2 * n,)),
+            dma((2 * n,)),
+            dma((n,)),
+            dma((n,)),
+            dma((n,)),
+            dma((n,)),
+            dma((n,)),
+            dma((n,)),
+        ],
+        compiler_params=pltpu.CompilerParams(
+            collective_id=0, has_side_effects=True, vmem_limit_bytes=44 * 2**20
+        ),
+    )(
+        pre,
+        token_input.reshape(rows, cols),
+        gate_input.reshape(rows, cols),
+        vecs,
+        target[:, None],
+        target[None],
+        query_rows,
+        fresh,
+        bias,
+        fresh_bias,
+        ssm_state,
+        kv,
+        proj_weight,
+        dt_weight,
+        decay_log,
+    )
+    return mamba.reshape(total, STEPS, cols), attended.reshape(total, STEPS, acols)
+
+
 def solution(mesh):
     in_specs = (
         P(("groups", "req"), None, "tp"),
@@ -157,4 +613,6 @@
         P("groups"),
     )
     out_specs = (P("groups", None, ("tp", "req")), P("groups", None, ("tp", "req")))
-    return jax.shard_map(local, mesh=mesh, in_specs=in_specs, out_specs=out_specs, check_vma=False)
+    kernel_fits = mesh.shape["req"] <= 8 and mesh.shape["tp"] == 2
+    body = local_kernel if kernel_fits else local
+    return jax.shard_map(body, mesh=mesh, in_specs=in_specs, out_specs=out_specs, check_vma=False)

time: 268 us -> 74.3 us (0.28)
  waiting for transfers between devices: 92.2 us -> 0 us
  local copies, waits for them, and re-layouts: 101 us -> 21.9 us
  Pallas kernels: 0 us -> 45.9 us
  starting transfers between devices: 34.8 us -> 0 us
  between operations: 14.5 us -> 0.75 us
  matrix products: 10.2 us -> 0 us
  other arithmetic: 13.9 us -> 5.06 us
    psum x1 -> x0, waiting for transfers between devices: 83.6 us -> none  [project(): return lax.psum(partial_sum, ('req', 'tp'))]
    pallas_call x0 -> x1, Pallas kernels: none -> 45.9 us  [local_kernel(): pl.pallas_call(functools.partial(block_kernel, n, slots, cols, acols, kv_...]
    all_to_all x6 -> x0, starting transfers between devices: 34.8 us -> none  [the longest x1 7.28 us: local(): lax.all_to_all(token_input[decode_row], 'req', split_axis=0, concat_axis=...]
    all_to_all x7 -> x0, local copies, waits for them, and re-layouts: 24.9 us -> none  [the longest x1 9.49 us: local(): lax.all_to_all(result, 'req', split_axis=2, concat_axis=0, tiled=True)]
    unnamed x58 -> x19, local copies, waits for them, and re-layouts: 32.8 us -> 9.65 us
    another operation x6 -> x0, local copies, waits for them, and re-layouts: 17.6 us -> none  [the longest x1 6.72 us: advance(): return jnp.stack(results, axis=1)]
    gather x6 -> x0, local copies, waits for them, and re-layouts: 12.4 us -> none  [the longest x1 2.73 us: local(): token_input[decode_row]]
    dot_general x6 -> x0, matrix products: 10.2 us -> none  [the longest x1 3.06 us: attend(): jnp.einsum('btkgd,bnkd->btkgn', queryq, keys, preferred_element_type=jnp....]
  transfers between devices with their start and end apart: 7 -> 0, of which waited for: 2 -> 0; matrix products, arithmetic and copies ran while one was open for 33% -> 0% of each run, Pallas kernels for 0% -> 0%
where the time goes in v1:
time: 74.3 us; the launch traced here: 73.6 us
  Pallas kernels  45.9 us (62%)
  local copies, waits for them, and re-layouts  21.9 us (29%)
  other arithmetic  5.06 us (7%)
  between operations  0.75 us (1%)
    pallas_call x1, Pallas kernels, local_kernel(): pl.pallas_call(functools.partial(block_kernel, n, slots, cols, acols, kv_...  45.9 us
    unnamed x19, local copies, waits for them, and re-layouts  9.65 us
    reshape x1, local copies, waits for them, and re-layouts, local_kernel(): mamba.reshape(total, STEPS, cols)  1.75 us
    transpose x1, local copies, waits for them, and re-layouts, local_kernel(): query_rows = queries.transpose(1, 0, 2).reshape(STEPS * slots, -1)  1.64 us
    reshape x1, local copies, waits for them, and re-layouts, local_kernel(): attended.reshape(total, STEPS, acols)  1.61 us

profile of v1, /device:TPU:0, one launch (start us, length us, event | category | flops | bytes accessed | tf_op | source)
XLA Modules:
  0.0 73.6 jit_solution(16716078088274671768)
XLA Ops:
  0.6 0.8 %select_reduce_fusion = s32[128]{0:T(128)S(1)} fusion(s32[128]{0:T(128)} %bitcast.51), kind=kLoop, calls=%fused_computation.14 | loop fusion | flops 49024 | bytes 1024 | tf_op jit(solution)/shard_map/reduce_sum | solution.py:498
  1.4 0.7 broadcast_multiply_fusion
  2.1 0.1 mul.78
  2.2 0.1 add.127.perm_row_ref
  2.3 0.7 fusion.5
  3.0 0.1 and_select_fusion.fresh_bias_ref
  3.1 1.4 %copy.34 = bf16[2,2,8,512]{3,2,1,0:T(8,128)(2,1)} copy(bf16[2,2,8,512]{3,0,1,2:T(2,128)(2,1)} %bitcast.48) | data formatting | bytes 65536 | tf_op jit(solution)/shard_map/transpose | solution.py:518
  4.4 0.7 add.135.perm_col_ref
  5.1 0.1 add.129
  5.2 0.1 add.130
  5.3 0.0 copy-start.1
  5.3 1.0 %slice.31 = f32[2,8192]{1,0:T(2,128)S(1)} slice(f32[4,8192]{1,0:T(4,128)} %param.21), slice={[2:4], [0:8192]} | slice | bytes 131072 | tf_op jit(solution)/shard_map/slice | solution.py:494
  6.3 0.9 %pad_maximum_fusion.1.vec_ref = f32[4,8192]{1,0:T(4,128)S(1)} fusion(f32[1,8192]{1,0:T(1,128)} %bitcast.49, f32[1,8192]{1,0:T(1,128)} %bitcast.50, f32[2,8192]{1,0:T(2,128)S(1)} %slice.31), kind=kLoop, calls=%fused_computation.11 | loop fusion | flops 65536 | bytes 262144 | tf_op jit(solution)/shard_map/concatenate | solution.py:494
  7.2 0.1 add.132
  7.3 1.2 %fusion.7 = (f32[1,8192]{1,0:T(1,128)S(1)}, f32[1,8192]{1,0:T(1,128)S(1)}, f32[1,8192]{1,0:T(1,128)S(1)}) fusion(f32[4,8192]{1,0:T(4,128)} %param.21), kind=kLoop, calls=%fused_computation.34 | loop fusion | bytes 196608 | tf_op jit(solution)/shard_map/slice | solution.py:490
  8.5 1.6 %copy.33 = bf16[2,8,4096]{2,1,0:T(8,128)(2,1)} copy(bf16[2,8,4096]{2,0,1:T(2,128)(2,1)} %bitcast.44) | data formatting | bytes 262144 | tf_op jit(solution)/shard_map/transpose | solution.py:517
  10.1 1.0 %reshape.215.tok_ref = bf16[128,1024]{1,0:T(8,128)(2,1)S(1)} reshape(bf16[64,2,1024]{2,1,0:T(2,128)(2,1)} %param.19) | data formatting | bytes 524288 | tf_op jit(solution)/shard_map/reshape | solution.py:577
  11.2 1.1 %reshape.216.gate_ref = bf16[128,1024]{1,0:T(8,128)(2,1)S(1)} reshape(bf16[64,2,1024]{2,1,0:T(2,128)(2,1)} %param.20) | data formatting | bytes 524288 | tf_op jit(solution)/shard_map/reshape | solution.py:578
  12.2 1.2 %fusion = (f32[8,8192]{1,0:T(8,128)S(1)}, f32[8,8192]{1,0:T(8,128)S(1)}) fusion(f32[8,3,8192]{2,0,1:T(8,128)} %param.18, f32[8192]{0:T(1024)S(1)} %bitcast.45, f32[8192]{0:T(1024)S(1)} %bitcast.46, f32[8192]{0:T(1024)S(1)} %bitcast.47, f32[8192]{0:T(1024)} %param.22), kind=kLoop, calls=%fused_computation.3 | loop fusion | flops 655360 | bytes 1441792 | tf_op jit(solution)/shard_map/add | solution.py:487
  13.5 0.2 lt.32
  13.7 0.3 lt.33
  14.0 0.7 pad_maximum_fusion.2.bias_ref
  14.6 1.7 %copy.30.pw_hbm = bf16[1024,544]{1,0:T(8,128)(2,1)S(1)} copy(bf16[1024,544]{0,1:T(8,128)(2,1)} %param.23) | data formatting | bytes 2228224 | tf_op args[6]
  16.3 0.0 copy-done.1
  16.3 0.0 copy-start
  16.3 2.2 %copy-done = f32[8,16,8192]{2,1,0:T(8,128)S(1)} copy-done((f32[8,16,8192]{2,1,0:T(8,128)S(1)}, f32[8,16,8192]{2,1,0:T(8,128)}, u32[]{:S(2)}) %copy-start) | copy-done | bytes 4194328
  18.5 0.0 copy-start.2
  18.5 0.9 %copy-done.2 = bf16[2,8,4096]{2,1,0:T(8,128)(2,1)S(1)} copy-done((bf16[2,8,4096]{2,1,0:T(8,128)(2,1)S(1)}, bf16[2,8,4096]{2,1,0:T(8,128)(2,1)}, u32[]{:S(2)}) %copy-start.2) | copy-done | bytes 131096
  19.4 0.0 copy-start.3
  19.4 0.9 %copy-done.3 = f32[16,2048]{1,0:T(8,128)S(1)} copy-done((f32[16,2048]{1,0:T(8,128)S(1)}, f32[16,2048]{1,0:T(8,128)}, u32[]{:S(2)}) %copy-start.3) | copy-done | bytes 131096
  20.3 0.0 copy-start.4
  20.3 1.0 %copy-done.4 = f32[16,8192]{1,0:T(8,128)S(1)} copy-done((f32[16,8192]{1,0:T(8,128)S(1)}, f32[16,8192]{1,0:T(8,128)}, u32[]{:S(2)}) %copy-start.4) | copy-done | bytes 524312
  21.4 0.0 copy-start.5
  21.4 0.8 %copy-done.5 = s32[128,1]{1,0:T(8,128)S(1)} copy-done((s32[128,1]{1,0:T(8,128)S(1)}, s32[128,1]{1,0:T(8,128)}, u32[]{:S(2)}) %copy-start.5) | copy-done | bytes 536
  22.2 0.0 copy-start.7
  22.2 0.8 %copy-done.7 = bf16[2,2,8,512]{3,2,1,0:T(8,128)(2,1)S(1)} copy-done((bf16[2,2,8,512]{3,2,1,0:T(8,128)(2,1)S(1)}, bf16[2,2,8,512]{3,2,1,0:T(8,128)(2,1)}, u32[]{:S(2)}) %copy-start.7) | copy-done | bytes 32792
  23.0 45.9 %shard_map.176 = (bf16[128,1024]{1,0:T(8,128)(2,1)S(1)}, bf16[128,512]{1,0:T(8,128)(2,1)S(1)}) custom-call(f32[16,8192]{1,0:T(8,128)S(1)} %pad_maximum_fusion.pre_ref, bf16[128,1024]{1,0:T(8,128)(2,1)S(1)} %reshape.215.tok_ref, bf16[128,1024]{1,0:T(8,128)(2,1)S(1)} %reshape.216.gate_ref, f32[4,8192]{1,0:T(4,128)S(1)} %pad_maximum_fusion.1.vec_ref, ...), custom_call_target="tpu_custom_call" | custom-call | tf_op jit(solution)/shard_map/pallas_call | solution.py:525
  68.9 0.0 copy-start.6
  68.9 0.7 copy-done.6
  69.6 0.0 copy-start.8
  69.6 0.6 copy-done.8
  70.2 1.7 %reshape.220 = bf16[64,2,1024]{2,1,0:T(2,128)(2,1)} reshape(bf16[128,1024]{1,0:T(8,128)(2,1)} %copy-done.6) | data formatting | bytes 524288 | tf_op jit(solution)/shard_map/reshape | solution.py:592
  72.0 1.6 %reshape.221 = bf16[64,2,512]{2,1,0:T(2,128)(2,1)} reshape(bf16[128,512]{1,0:T(8,128)(2,1)} %copy-done.8) | data formatting | bytes 262144 | tf_op jit(solution)/shard_map/reshape | solution.py:592
  (7 shorter events, 0.1 us)
Async XLA Ops:
  5.3 11.0 %copy-start.1 = (bf16[512,1024]{1,0:T(8,128)(2,1)S(1)}, bf16[512,1024]{1,0:T(8,128)(2,1)}, u32[]{:S(2)}) copy-start(bf16[512,1024]{1,0:T(8,128)(2,1)} %dtw_hbm.1) | copy-start | bytes 3145732
  16.3 2.2 %copy-start = (f32[8,16,8192]{2,1,0:T(8,128)S(1)}, f32[8,16,8192]{2,1,0:T(8,128)}, u32[]{:S(2)}) copy-start(f32[8,16,8192]{2,1,0:T(8,128)} %state_hbm.1) | copy-start | bytes 12582916
  18.5 0.9 %copy-start.2 = (bf16[2,8,4096]{2,1,0:T(8,128)(2,1)S(1)}, bf16[2,8,4096]{2,1,0:T(8,128)(2,1)}, u32[]{:S(2)}) copy-start(bf16[2,8,4096]{2,1,0:T(8,128)(2,1)} %copy.33) | copy-start | bytes 393220
  19.4 0.9 %copy-start.3 = (f32[16,2048]{1,0:T(8,128)S(1)}, f32[16,2048]{1,0:T(8,128)}, u32[]{:S(2)}) copy-start(f32[16,2048]{1,0:T(8,128)} %pad_maximum_fusion.2.bias_ref) | copy-start | bytes 393220
  20.3 1.0 %copy-start.4 = (f32[16,8192]{1,0:T(8,128)S(1)}, f32[16,8192]{1,0:T(8,128)}, u32[]{:S(2)}) copy-start(f32[16,8192]{1,0:T(8,128)} %decay_hbm.1) | copy-start | bytes 1572868
  21.4 0.8 %copy-start.5 = (s32[128,1]{1,0:T(8,128)S(1)}, s32[128,1]{1,0:T(8,128)}, u32[]{:S(2)}) copy-start(s32[128,1]{1,0:T(8,128)} %add.135.perm_col_ref) | copy-start | bytes 1540
  22.2 0.8 %copy-start.7 = (bf16[2,2,8,512]{3,2,1,0:T(8,128)(2,1)S(1)}, bf16[2,2,8,512]{3,2,1,0:T(8,128)(2,1)}, u32[]{:S(2)}) copy-start(bf16[2,2,8,512]{3,2,1,0:T(8,128)(2,1)} %copy.34) | copy-start | bytes 98308
  68.9 0.7 copy-start.6
  69.6 0.6 copy-start.8

commit v2 on v1

--- a/solution.py
+++ b/solution.py
@@ -148,28 +148,43 @@
     cols,
     acols,
     kv_heads,
-    pre_ref,
-    tok_ref,
-    gate_ref,
-    vec_ref,
-    perm_col_ref,
-    perm_row_ref,
-    query_ref,
-    fresh_ref,
-    bias_ref,
-    fresh_bias_ref,
-    state_hbm,
     kv_hbm,
+    query_hbm,
+    fresh_hbm,
     pw_hbm,
     dtw_hbm,
+    state_hbm,
     decay_hbm,
+    gate_hbm,
+    dt_bias_hbm,
+    skip_hbm,
+    conv_hbm,
+    taps_hbm,
+    conv_bias_hbm,
+    tok_hbm,
+    row_ref,
+    table_ref,
+    len_ref,
     mamba_ref,
     att_ref,
-    state,
     kv,
+    query_in,
+    fresh_in,
     pw,
     dtw,
+    state,
     decay,
+    gate_in,
+    dt_bias,
+    skip_gain,
+    conv,
+    taps,
+    conv_bias,
+    tok_in,
+    pre,
+    bias,
+    query,
+    fresh_ref,
     pre_send,
     pre_recv,
     tok_send,
@@ -210,11 +225,24 @@
     rows = n * ROWS
     f32, bf16 = jnp.float32, jnp.bfloat16
 
+    pairs = (
+        (conv_hbm, conv),
+        (taps_hbm, taps),
+        (conv_bias_hbm, conv_bias),
+        (tok_hbm, tok_in),
+        (query_hbm, query_in),
+        (fresh_hbm, fresh_in),
+        (kv_hbm, kv),
+        (pw_hbm, pw),
+        (dt_bias_hbm, dt_bias),
+        (dtw_hbm, dtw),
+        (state_hbm, state),
+        (decay_hbm, decay),
+        (skip_hbm, skip_gain),
+        (gate_hbm, gate_in),
+    )
     loads = [
-        pltpu.make_async_copy(src, dst, load_sem.at[i])
-        for i, (src, dst) in enumerate(
-            ((kv_hbm, kv), (pw_hbm, pw), (dtw_hbm, dtw), (state_hbm, state), (decay_hbm, decay))
-        )
+        pltpu.make_async_copy(src, dst, load_sem.at[i]) for i, (src, dst) in enumerate(pairs)
     ]
     for load in loads:
         load.start()
@@ -269,11 +297,42 @@
             device_id_type=pl.DeviceIdType.MESH,
         )
 
-    for j in range(n):
-        pre_send[j] = pre_ref[:, j * cols : (j + 1) * cols].astype(bf16)
-    lane = lax.broadcasted_iota(jnp.int32, (rows, rows), 1)
-    perm = jnp.where(perm_col_ref[...] == lane, 1.0, 0.0).astype(bf16)
-    tok = jnp.dot(perm, tok_ref[...], preferred_element_type=f32)
+    for load in loads[:3]:
+        load.wait()
+
+    @pl.loop(0, n)
+    def _(j):
+        block = pl.ds(pl.multiple_of(j * cols, cols), cols)
+        w = [taps[i : i + 1, block] for i in range(CONV)]
+        oldest, older, last = conv[0, :, block], conv[1, :, block], conv[2, :, block]
+        base = conv_bias[:, block]
+        first = base + oldest * w[0] + older * w[1] + last * w[2]
+        second = base + older * w[0] + last * w[1]
+        both = jnp.concatenate([first, second], axis=0)
+        pre[:, block] = both
+        pre_send[pl.ds(j, 1)] = both.astype(bf16)[None]
+
+    def iota(shape, axis):
+        return lax.broadcasted_iota(jnp.int32, shape, axis)
+
+    def hot(condition):
+        return jnp.where(condition, 1.0, 0.0).astype(bf16)
+
+    requests = n * slots
+    where_row = hot(row_ref[...] == iota((rows, requests), 0) // STEPS)
+    column = iota((requests, rows), 1)
+    slot_of = column // ROWS * slots + column % slots
+    spread = hot(slot_of == iota((requests, rows), 0))
+    same_step = iota((rows, rows), 1) % ROWS // slots == iota((rows, rows), 0) % STEPS
+    back = jnp.dot(where_row, spread, preferred_element_type=f32)
+    back = jnp.where(same_step, back, 0.0).astype(bf16)
+    loads[3].wait()
+    tok = lax.dot_general(
+        back,
+        tok_in[...].reshape(rows, cols),
+        (((0,), (0,)), ((), ())),
+        preferred_element_type=f32,
+    )
     tok_send[...] = tok.astype(bf16).reshape(n, ROWS, cols)
 
     pl.semaphore_wait(barrier, total - 1)
@@ -282,7 +341,48 @@
     pre_recv[pl.ds(me, 1)] = pre_send[pl.ds(me, 1)]
     tok_recv[pl.ds(me, 1)] = tok_send[pl.ds(me, 1)]
 
-    loads[0].wait()
+    pages = table_ref.shape[1]
+    page = kv.shape[1] // pages
+    per_slot = pages // slots
+    lens = jnp.sum(
+        jnp.where(
+            iota((slots, slots), 0) == iota((slots, slots), 1), len_ref[...].astype(f32), 0.0
+        ),
+        axis=1,
+        keepdims=True,
+    )
+    entry = iota((slots, pages), 1)
+    counts = lens - (entry % per_slot * page).astype(f32)
+    counts = jnp.where(
+        entry // per_slot == iota((slots, pages), 0), jnp.clip(counts, 0.0, float(page)), 0.0
+    )
+    held = hot(table_ref[...] == iota((pages, pages), 0))
+    counts = lax.dot_general(
+        counts.astype(bf16), held, (((1,), (1,)), ((), ())), preferred_element_type=f32
+    )
+    widen = hot(iota((pages, pages * page), 1) // page == iota((pages, pages * page), 0))
+    counts = jnp.dot(counts.astype(bf16), widen, preferred_element_type=f32)
+    token = (iota((slots, pages * page), 1) % page).astype(f32)
+    live = jnp.where(token < counts, 0.0, -1e30)
+    bias[...] = jnp.concatenate([live] * STEPS, axis=0)
+    turned = (iota((ROWS, ROWS), 0) % slots) * STEPS + iota((ROWS, ROWS), 0) // slots
+    turn = hot(turned == iota((ROWS, ROWS), 1))
+    for load in loads[4:7]:
+        load.wait()
+    query[...] = jnp.dot(
+        turn, query_in[...].reshape(ROWS, -1), preferred_element_type=f32
+    ).astype(bf16)
+    row32, col32 = iota((2 * ROWS, 2 * ROWS), 0), iota((2 * ROWS, 2 * ROWS), 1)
+    pick = (row32 % slots) * 2 * STEPS + (row32 % ROWS) // slots * 2 + row32 // ROWS
+    fresh = jnp.dot(
+        hot(pick == col32),
+        fresh_in[...].reshape(2 * ROWS, -1),
+        preferred_element_type=f32,
+    ).astype(bf16)
+    row16, col16 = iota((ROWS, ROWS), 0), iota((ROWS, ROWS), 1)
+    allowed = (row16 % slots == col16 % slots) & (col16 // slots <= row16 // slots)
+    fresh_bias = jnp.where(allowed, 0.0, -1e30)
+    fresh_ref[...] = fresh.reshape(2, ROWS, -1)
     group = (acols * n) // (kv_heads * HD)
     per_block = acols // HD
     scale = 1.0 / math.sqrt(HD)
@@ -293,7 +393,7 @@
         lanes = pl.ds(pl.multiple_of(h * HD, HD), HD)
         q = jnp.concatenate(
             [
-                query_ref[:, pl.ds(pl.multiple_of((h * group + g) * HD, HD), HD)]
+                query[:, pl.ds(pl.multiple_of((h * group + g) * HD, HD), HD)]
                 for g in range(group)
             ],
             axis=0,
@@ -302,8 +402,8 @@
         new = lax.dot_general(
             q, fresh_ref[0, :, lanes], contract, preferred_element_type=f32
         )
-        old = old.reshape(group, ROWS, -1) * scale + bias_ref[...][None]
-        new = new.reshape(group, ROWS, -1) * scale + fresh_bias_ref[...][None]
+        old = old.reshape(group, ROWS, -1) * scale + bias[...][None]
+        new = new.reshape(group, ROWS, -1) * scale + fresh_bias[None]
         top = jnp.maximum(
             jnp.max(old, axis=-1, keepdims=True), jnp.max(new, axis=-1, keepdims=True)
         )
@@ -320,20 +420,21 @@
             att_send[h * (group // per_block) + g // per_block, :, place * HD : (place + 1) * HD] = out[g]
 
     here = pl.ds(pl.multiple_of(me * cols, cols), cols)
-    taps = vec_ref[0:2, here]
-    bias_cols = vec_ref[2:3, here]
+    w2, w3 = taps[2:3, here], taps[3:4, here]
     tok4 = tok.reshape(n, 2, 8, cols)
     req_wait(pre_send, pre_recv, pre_ss, pre_rs)
     pre4 = pre_recv[...].astype(f32).reshape(n, 2, 8, cols)
-    first = pre4[:, 0] + tok4[:, 0] * taps[1:2][None]
-    second = pre4[:, 1] + tok4[:, 0] * taps[0:1][None] + tok4[:, 1] * taps[1:2][None]
+    first = pre4[:, 0] + tok4[:, 0] * w3[None]
+    second = pre4[:, 1] + tok4[:, 0] * w2[None] + tok4[:, 1] * w3[None]
     mixed = jnp.stack([jax.nn.silu(first), jax.nn.silu(second)], axis=1)
     mixed = mixed.reshape(rows, cols).astype(bf16)
-    loads[1].wait()
-    part = jnp.dot(mixed, pw[...], preferred_element_type=f32)
+    loads[7].wait()
+    part = lax.dot_general(mixed, pw[...], contract, preferred_element_type=f32)
     half = DT_RANK // 2
+    maps = part[:, DT_RANK:]
+    upper = maps.astype(bf16).astype(f32)
     maps = jnp.concatenate(
-        [part[:, DT_RANK:], jnp.zeros((rows, 128 - 2 * STATE), f32)], axis=1
+        [upper, maps - upper, jnp.zeros((rows, 128 - 4 * STATE), f32)], axis=1
     )
     for c in range(2):
         part_send[c * n : (c + 1) * n, :, :half] = (
@@ -367,8 +468,10 @@
     square = jnp.concatenate(
         [summed[:, half:], jnp.zeros((128 - ROWS, 128), f32)], axis=0
     )
-    maps_t[...] = jnp.transpose(square)[: 2 * STATE]
-    loads[2].wait()
+    flipped = jnp.transpose(square)
+    maps_t[...] = flipped[: 2 * STATE] + flipped[2 * STATE : 4 * STATE]
+    loads[8].wait()
+    loads[9].wait()
 
     @pl.loop(1, total)
     def _(k):
@@ -377,7 +480,7 @@
 
     z = jnp.dot(low_recv[:n].reshape(rows, half), dtw[:half], preferred_element_type=f32)
     z = z + jnp.dot(low_recv[n:].reshape(rows, half), dtw[half:], preferred_element_type=f32)
-    zbuf[...] = (z + bias_cols).reshape(n, ROWS, cols)
+    zbuf[...] = (z + dt_bias[:, here]).reshape(n, ROWS, cols)
 
     @pl.loop(0, n)
     def _(k):
@@ -391,8 +494,8 @@
             req_copy(del_send, del_recv, del_ss, del_rs, peer, me).start()
 
     del_recv[pl.ds(me, 1)] = del_send[pl.ds(me, 1)]
-    loads[3].wait()
-    loads[4].wait()
+    for load in loads[10:13]:
+        load.wait()
     req_wait(tok_send, tok_recv, tok_ss, tok_rs)
 
     @pl.loop(0, n)
@@ -406,11 +509,11 @@
         block = pl.ds(pl.multiple_of(peer * cols, cols), cols)
         delta = del_recv[peer].astype(f32)
         toks = tok_recv[peer].astype(f32)
-        w2 = vec_ref[0:1, block]
-        w3 = vec_ref[1:2, block]
-        skip = vec_ref[3:4, block]
-        x0 = pre_ref[0:8, block] + toks[0:8] * w3
-        x1 = pre_ref[8:16, block] + toks[0:8] * w2 + toks[8:16] * w3
+        w2 = taps[2:3, block]
+        w3 = taps[3:4, block]
+        skip = skip_gain[:, block]
+        x0 = pre[0:8, block] + toks[0:8] * w3
+        x1 = pre[8:16, block] + toks[0:8] * w2 + toks[8:16] * w3
         x = jnp.concatenate([jax.nn.silu(x0), jax.nn.silu(x1)], axis=0)
         x = x.astype(bf16).astype(f32)
         dx = delta * x
@@ -431,15 +534,14 @@
 
     val_recv[pl.ds(me, 1)] = val_send[pl.ds(me, 1)]
 
-    sub = lax.broadcasted_iota(jnp.int32, (rows, rows), 0)
-    back = jnp.where(perm_row_ref[...] == sub, 1.0, 0.0).astype(bf16)
-    gate = jax.nn.silu(gate_ref[...].astype(f32))
+    loads[13].wait()
+    gate = jax.nn.silu(gate_in[...].reshape(rows, cols).astype(f32))
     req_wait(att_send, att_recv, att_ss, att_rs)
     att = jnp.dot(back, att_recv[...].reshape(rows, acols), preferred_element_type=f32)
-    att_ref[...] = att.astype(bf16)
+    att_ref[...] = att.astype(bf16).reshape(att_ref.shape)
     req_wait(val_send, val_recv, val_ss, val_rs)
     val = jnp.dot(back, val_recv[...].reshape(rows, cols), preferred_element_type=f32)
-    mamba_ref[...] = (val * gate).astype(bf16)
+    mamba_ref[...] = (val * gate).astype(bf16).reshape(mamba_ref.shape)
 
     req_drain(pre_send, pre_recv, pre_ss, pre_rs)
     req_drain(tok_send, tok_recv, tok_ss, tok_rs)
@@ -481,41 +583,7 @@
     acols = queries.shape[2] // n
     kv_heads = KVH // lax.axis_size("tp")
     pages, page = kv_pages.shape[1:3]
-    per_slot = pages // slots
     rows = total * STEPS
-    pre0 = (
-        conv_bias
-        + conv_state[:, 0] * conv_weight[0]
-        + conv_state[:, 1] * conv_weight[1]
-        + conv_state[:, 2] * conv_weight[2]
-    )
-    pre1 = conv_bias + conv_state[:, 1] * conv_weight[0] + conv_state[:, 2] * conv_weight[1]
-    pre = jnp.concatenate([pre0, pre1], axis=0)
-    vecs = jnp.concatenate([conv_weight[2:4], dt_bias[None], skip_gain[None]], axis=0)
-    target = (
-        decode_row.reshape(n, 1, slots) * STEPS + jnp.arange(STEPS, dtype=jnp.int32)[None, :, None]
-    ).reshape(rows)
-    entry = jnp.sum(
-        jnp.where(
-            page_table.reshape(-1, 1) == jnp.arange(pages)[None],
-            jnp.arange(pages, dtype=jnp.int32)[:, None],
-            0,
-        ),
-        axis=0,
-    )
-    place = (entry % per_slot)[:, None] * page + jnp.arange(page)[None]
-    limit = jnp.where(
-        (entry // per_slot)[None] == jnp.arange(slots)[:, None], context_len[:, None], 0
-    )
-    live = (place[None] < limit[:, :, None]).reshape(slots, pages * page)
-    bias = jnp.where(live, 0.0, -1e30).astype(jnp.float32)
-    bias = jnp.concatenate([bias] * STEPS, axis=0)
-    index = jnp.arange(STEPS * slots)
-    own = (index % slots)[:, None] == (index % slots)[None]
-    causal = (index // slots)[None] <= (index // slots)[:, None]
-    fresh_bias = jnp.where(own & causal, 0.0, -1e30).astype(jnp.float32)
-    query_rows = queries.transpose(1, 0, 2).reshape(STEPS * slots, -1)
-    fresh = new_kv.transpose(2, 1, 0, 3).reshape(2, STEPS * slots, -1)
     kv = kv_pages.reshape(2, pages * page, -1)
     half = DT_RANK // 2
     bf16, f32 = jnp.bfloat16, jnp.float32
@@ -525,17 +593,30 @@
     mamba, attended = pl.pallas_call(
         functools.partial(block_kernel, n, slots, cols, acols, kv_heads),
         out_shape=(
-            jax.ShapeDtypeStruct((rows, cols), bf16),
-            jax.ShapeDtypeStruct((rows, acols), bf16),
+            jax.ShapeDtypeStruct((total, STEPS, cols), bf16),
+            jax.ShapeDtypeStruct((total, STEPS, acols), bf16),
         ),
-        in_specs=[vmem] * 10 + [hbm] * 5,
+        in_specs=[hbm] * 14 + [vmem] * 3,
         out_specs=(vmem, vmem),
         scratch_shapes=[
+            pltpu.VMEM(kv.shape, bf16),
+            pltpu.VMEM(queries.shape, bf16),
+            pltpu.VMEM(new_kv.shape, bf16),
+            pltpu.VMEM(proj_weight.shape[::-1], bf16),
+            pltpu.VMEM(dt_weight.shape, bf16),
             pltpu.VMEM(ssm_state.shape, f32),
-            pltpu.VMEM(kv.shape, bf16),
-            pltpu.VMEM(proj_weight.shape, bf16),
-            pltpu.VMEM(dt_weight.shape, bf16),
             pltpu.VMEM(decay_log.shape, f32),
+            pltpu.VMEM(gate_input.shape, bf16),
+            pltpu.VMEM((1, width), f32),
+            pltpu.VMEM((1, width), f32),
+            pltpu.VMEM((CONV - 1, slots, width), f32),
+            pltpu.VMEM(conv_weight.shape, f32),
+            pltpu.VMEM((1, width), f32),
+            pltpu.VMEM(token_input.shape, bf16),
+            pltpu.VMEM((ROWS, width), f32),
+            pltpu.VMEM((ROWS, pages * page), f32),
+            pltpu.VMEM((ROWS, queries.shape[2]), bf16),
+            pltpu.VMEM((2, ROWS, new_kv.shape[3]), bf16),
             pltpu.VMEM((n, ROWS, cols), bf16),
             pltpu.VMEM((n, ROWS, cols), bf16),
             pltpu.VMEM((n, ROWS, cols), bf16),
@@ -553,7 +634,7 @@
             pltpu.VMEM((n, ROWS, cols), f32),
             pltpu.VMEM((ROWS, cols), f32),
             pltpu.VMEM((2 * STATE, 128), f32),
-            dma((5,)),
+            dma((14,)),
             dma((n,)),
             dma((n,)),
             dma((n,)),
@@ -570,26 +651,28 @@
             dma((n,)),
         ],
         compiler_params=pltpu.CompilerParams(
-            collective_id=0, has_side_effects=True, vmem_limit_bytes=44 * 2**20
+            collective_id=0, has_side_effects=True, vmem_limit_bytes=60 * 2**20
         ),
     )(
-        pre,
-        token_input.reshape(rows, cols),
-        gate_input.reshape(rows, cols),
-        vecs,
-        target[:, None],
-        target[None],
-        query_rows,
-        fresh,
-        bias,
-        fresh_bias,
+        kv,
+        queries,
+        new_kv,
+        proj_weight.T,
+        dt_weight,
         ssm_state,
-        kv,
-        proj_weight,
-        dt_weight,
         decay_log,
-    )
-    return mamba.reshape(total, STEPS, cols), attended.reshape(total, STEPS, acols)
+        gate_input,
+        dt_bias[None],
+        skip_gain[None],
+        conv_state.transpose(1, 0, 2),
+        conv_weight,
+        conv_bias[None],
+        token_input,
+        decode_row[None],
+        page_table,
+        context_len[None],
+    )
+    return mamba, attended
 
 
 def solution(mesh):

time: 74.3 us -> 51.3 us (0.69)
  local copies, waits for them, and re-layouts: 21.9 us -> 3.48 us
  other arithmetic: 5.06 us -> 0 us
  Pallas kernels: 45.9 us -> 47 us
    unnamed x19 -> x2, local copies, waits for them, and re-layouts: 9.65 us -> 3.48 us
    reshape x4 -> x0, local copies, waits for them, and re-layouts: 5.46 us -> none  [the longest x1 1.75 us: local_kernel(): mamba.reshape(total, STEPS, cols)]
    transpose x2 -> x0, local copies, waits for them, and re-layouts: 3 us -> none  [the longest x1 1.64 us: local_kernel(): query_rows = queries.transpose(1, 0, 2).reshape(STEPS * slots, -1)]
    slice x2 -> x0, local copies, waits for them, and re-layouts: 2.18 us -> none  [the longest x1 1.15 us: local_kernel(): conv_weight[2]]
    concatenate x3 -> x0, other arithmetic: 1.57 us -> none  [the longest x1 0.87 us: local_kernel(): jnp.concatenate([conv_weight[2:4], dt_bias[None], skip_gain[None]], axis=0)]
    add x3 -> x0, other arithmetic: 1.25 us -> none  [the longest x1 1.24 us: local_kernel(): conv_bias + conv_state[:, 0] * conv_weight[0]]
    pallas_call x1, Pallas kernels: 45.9 us -> 47 us  [local_kernel(): pl.pallas_call(functools.partial(block_kernel, n, slots, cols, acols, kv_...]
    add x6 -> x0, local copies, waits for them, and re-layouts: 1.05 us -> none  [the longest x2 0.8 us: local_kernel(): decode_row.reshape(n, 1, slots) * STEPS]
where the time goes in v2:
time: 51.3 us; the launch traced here: 51.1 us
  Pallas kernels  47 us (92%)
  local copies, waits for them, and re-layouts  3.48 us (7%)
  between operations  0.65 us (1%)
    pallas_call x1, Pallas kernels, local_kernel(): pl.pallas_call(functools.partial(block_kernel, n, slots, cols, acols, kv_...  47 us
    unnamed x2, local copies, waits for them, and re-layouts  3.48 us

profile of v2, /device:TPU:0, one launch (start us, length us, event | category | flops | bytes accessed | tf_op | source)
XLA Modules:
  0.0 51.1 jit_solution(856640280077699738)
XLA Ops:
  0.6 47.0 %shard_map.176 = (bf16[64,2,1024]{2,1,0:T(2,128)(2,1)}, bf16[64,2,512]{2,1,0:T(2,128)(2,1)}) custom-call(bf16[2,2048,512]{2,1,0:T(8,128)(2,1)} %bitcast.8, bf16[8,2,4096]{2,1,0:T(2,128)(2,1)} %query_hbm.1, bf16[8,2,2,512]{3,2,1,0:T(2,128)(2,1)} %fresh_hbm.1, bf16[544,1024]{1,0:T(8,128)(2,1)} %bitcast.9, bf16[512,1024]{1,0:T(8,128)(2,1)} %dtw_hbm.1, ...), custom_call_target="tpu_custom_call" | custom-call | tf_op jit(solution)/shard_map/pallas_call | solution.py:593
  47.6 1.8 %copy.21 = bf16[64,2,1024]{2,1,0:T(2,128)(2,1)} copy(bf16[64,2,1024]{2,1,0:T(2,128)(2,1)} %get-tuple-element.4) | data formatting | bytes 524288
  49.5 1.6 %copy.22 = bf16[64,2,512]{2,1,0:T(2,128)(2,1)} copy(bf16[64,2,512]{2,1,0:T(2,128)(2,1)} %get-tuple-element.5) | data formatting | bytes 262144

commit v3 on v2

--- a/solution.py
+++ b/solution.py
@@ -337,7 +337,6 @@
 
     pl.semaphore_wait(barrier, total - 1)
     req_start(pre_send, pre_recv, pre_ss, pre_rs)
-    req_start(tok_send, tok_recv, tok_ss, tok_rs)
     pre_recv[pl.ds(me, 1)] = pre_send[pl.ds(me, 1)]
     tok_recv[pl.ds(me, 1)] = tok_send[pl.ds(me, 1)]
 
@@ -388,8 +387,7 @@
     scale = 1.0 / math.sqrt(HD)
     contract = (((1,), (1,)), ((), ()))
 
-    @pl.loop(0, kv_heads)
-    def _(h):
+    def attend_head(h):
         lanes = pl.ds(pl.multiple_of(h * HD, HD), HD)
         q = jnp.concatenate(
             [
@@ -419,10 +417,14 @@
             place = g % per_block
             att_send[h * (group // per_block) + g // per_block, :, place * HD : (place + 1) * HD] = out[g]
 
+    early = kv_heads // 2
+    pl.loop(0, early)(attend_head)
+
     here = pl.ds(pl.multiple_of(me * cols, cols), cols)
     w2, w3 = taps[2:3, here], taps[3:4, here]
     tok4 = tok.reshape(n, 2, 8, cols)
     req_wait(pre_send, pre_recv, pre_ss, pre_rs)
+    req_start(tok_send, tok_recv, tok_ss, tok_rs)
     pre4 = pre_recv[...].astype(f32).reshape(n, 2, 8, cols)
     first = pre4[:, 0] + tok4[:, 0] * w3[None]
     second = pre4[:, 1] + tok4[:, 0] * w2[None] + tok4[:, 1] * w3[None]
@@ -448,6 +450,7 @@
         all_copy(part_send.at[peer], part_recv, part_ss, part_rs, peer, flat).start()
 
     part_recv[pl.ds(flat, 1)] = part_send[pl.ds(flat, 1)]
+    pl.loop(early, kv_heads)(attend_head)
 
     @pl.loop(1, total)
     def _(k):
@@ -554,6 +557,15 @@
         peer = lax.rem(flat + k, total)
         all_copy(part_send.at[peer], part_recv, part_ss, part_rs, peer, flat).wait_send()
         all_copy(low_send, low_recv, low_ss, low_rs, peer, flat).wait_send()
+
+
+def place_kernel(mamba_in, att_in, mamba_out, att_out, sem):
+    first = pltpu.make_async_copy(mamba_in, mamba_out, sem.at[0])
+    second = pltpu.make_async_copy(att_in, att_out, sem.at[1])
+    first.start()
+    second.start()
+    first.wait()
+    second.wait()
 
 
 def local_kernel(
@@ -672,7 +684,17 @@
         page_table,
         context_len[None],
     )
-    return mamba, attended
+    return pl.pallas_call(
+        place_kernel,
+        out_shape=(
+            jax.ShapeDtypeStruct(mamba.shape, bf16),
+            jax.ShapeDtypeStruct(attended.shape, bf16),
+        ),
+        in_specs=[hbm] * 2,
+        out_specs=(hbm, hbm),
+        scratch_shapes=[dma((2,))],
+        compiler_params=pltpu.CompilerParams(vmem_limit_bytes=60 * 2**20),
+    )(mamba, attended)
 
 
 def solution(mesh):

time: 51.3 us -> 64.5 us (1.26)
  Pallas kernels: 47 us -> 63.7 us
  local copies, waits for them, and re-layouts: 3.48 us -> 0 us
    pallas_call x0 -> x1, Pallas kernels: none -> 13 us  [local_kernel(): pl.pallas_call(place_kernel, out_shape=(jax.ShapeDtypeStruct(mamba.shape,...]
    pallas_call x1, Pallas kernels: 47 us -> 50.7 us  [local_kernel(): pl.pallas_call(functools.partial(block_kernel, n, slots, cols, acols, kv_...]
    unnamed x2 -> x0, local copies, waits for them, and re-layouts: 3.48 us -> none
where the time goes in v3:
time: 64.5 us; the launch traced here: 64.4 us
  Pallas kernels  63.7 us (99%)
  between operations  0.65 us (1%)
    pallas_call x1, Pallas kernels, local_kernel(): pl.pallas_call(functools.partial(block_kernel, n, slots, cols, acols, kv_...  50.7 us
    pallas_call x1, Pallas kernels, local_kernel(): pl.pallas_call(place_kernel, out_shape=(jax.ShapeDtypeStruct(mamba.shape,...  13 us

profile of v3, /device:TPU:0, one launch (start us, length us, event | category | flops | bytes accessed | tf_op | source)
XLA Modules:
  0.0 64.4 jit_solution(1437017866521180966)
XLA Ops:
  0.6 50.7 %shard_map.176 = (bf16[64,2,1024]{2,1,0:T(2,128)(2,1)}, bf16[64,2,512]{2,1,0:T(2,128)(2,1)}) custom-call(bf16[2,2048,512]{2,1,0:T(8,128)(2,1)} %bitcast.8, bf16[8,2,4096]{2,1,0:T(2,128)(2,1)} %query_hbm.1, bf16[8,2,2,512]{3,2,1,0:T(2,128)(2,1)} %fresh_hbm.1, bf16[544,1024]{1,0:T(8,128)(2,1)} %bitcast.9, bf16[512,1024]{1,0:T(8,128)(2,1)} %dtw_hbm.1, ...), custom_call_target="tpu_custom_call" | custom-call | tf_op jit(solution)/shard_map/pallas_call | solution.py:605
  51.3 13.0 %shard_map.177 = (bf16[64,2,1024]{2,1,0:T(2,128)(2,1)}, bf16[64,2,512]{2,1,0:T(2,128)(2,1)}) custom-call(bf16[64,2,1024]{2,1,0:T(2,128)(2,1)} %get-tuple-element.4.mamba_in, bf16[64,2,512]{2,1,0:T(2,128)(2,1)} %get-tuple-element.5.att_in), custom_call_target="tpu_custom_call" | custom-call | tf_op jit(solution)/shard_map/pallas_call | solution.py:687

commit v4 on v2

--- a/solution.py
+++ b/solution.py
@@ -337,7 +337,6 @@
 
     pl.semaphore_wait(barrier, total - 1)
     req_start(pre_send, pre_recv, pre_ss, pre_rs)
-    req_start(tok_send, tok_recv, tok_ss, tok_rs)
     pre_recv[pl.ds(me, 1)] = pre_send[pl.ds(me, 1)]
     tok_recv[pl.ds(me, 1)] = tok_send[pl.ds(me, 1)]
 
@@ -388,8 +387,7 @@
     scale = 1.0 / math.sqrt(HD)
     contract = (((1,), (1,)), ((), ()))
 
-    @pl.loop(0, kv_heads)
-    def _(h):
+    def attend_head(h):
         lanes = pl.ds(pl.multiple_of(h * HD, HD), HD)
         q = jnp.concatenate(
             [
@@ -419,10 +417,14 @@
             place = g % per_block
             att_send[h * (group // per_block) + g // per_block, :, place * HD : (place + 1) * HD] = out[g]
 
+    early = kv_heads // 2
+    pl.loop(0, early)(attend_head)
+
     here = pl.ds(pl.multiple_of(me * cols, cols), cols)
     w2, w3 = taps[2:3, here], taps[3:4, here]
     tok4 = tok.reshape(n, 2, 8, cols)
     req_wait(pre_send, pre_recv, pre_ss, pre_rs)
+    req_start(tok_send, tok_recv, tok_ss, tok_rs)
     pre4 = pre_recv[...].astype(f32).reshape(n, 2, 8, cols)
     first = pre4[:, 0] + tok4[:, 0] * w3[None]
     second = pre4[:, 1] + tok4[:, 0] * w2[None] + tok4[:, 1] * w3[None]
@@ -448,6 +450,7 @@
         all_copy(part_send.at[peer], part_recv, part_ss, part_rs, peer, flat).start()
 
     part_recv[pl.ds(flat, 1)] = part_send[pl.ds(flat, 1)]
+    pl.loop(early, kv_heads)(attend_head)
 
     @pl.loop(1, total)
     def _(k):

time: 51.3 us -> 55 us (1.072)
  Pallas kernels: 47 us -> 50.7 us
    pallas_call x1, Pallas kernels: 47 us -> 50.7 us  [local_kernel(): pl.pallas_call(functools.partial(block_kernel, n, slots, cols, acols, kv_...]
where the time goes in v4:
time: 55 us; the launch traced here: 54.8 us
  Pallas kernels  50.7 us (92%)
  local copies, waits for them, and re-layouts  3.48 us (6%)
  between operations  0.65 us (1%)
    pallas_call x1, Pallas kernels, local_kernel(): pl.pallas_call(functools.partial(block_kernel, n, slots, cols, acols, kv_...  50.7 us
    unnamed x2, local copies, waits for them, and re-layouts  3.48 us

profile of v4, /device:TPU:0, one launch (start us, length us, event | category | flops | bytes accessed | tf_op | source)
XLA Modules:
  0.0 54.8 jit_solution(480915733116621308)
XLA Ops:
  0.6 50.7 %shard_map.176 = (bf16[64,2,1024]{2,1,0:T(2,128)(2,1)}, bf16[64,2,512]{2,1,0:T(2,128)(2,1)}) custom-call(bf16[2,2048,512]{2,1,0:T(8,128)(2,1)} %bitcast.8, bf16[8,2,4096]{2,1,0:T(2,128)(2,1)} %query_hbm.1, bf16[8,2,2,512]{3,2,1,0:T(2,128)(2,1)} %fresh_hbm.1, bf16[544,1024]{1,0:T(8,128)(2,1)} %bitcast.9, bf16[512,1024]{1,0:T(8,128)(2,1)} %dtw_hbm.1, ...), custom_call_target="tpu_custom_call" | custom-call | tf_op jit(solution)/shard_map/pallas_call | solution.py:596
  51.3 1.8 %copy.21 = bf16[64,2,1024]{2,1,0:T(2,128)(2,1)} copy(bf16[64,2,1024]{2,1,0:T(2,128)(2,1)} %get-tuple-element.4) | data formatting | bytes 524288
  53.2 1.6 %copy.22 = bf16[64,2,512]{2,1,0:T(2,128)(2,1)} copy(bf16[64,2,512]{2,1,0:T(2,128)(2,1)} %get-tuple-element.5) | data formatting | bytes 262144
